TPU v7x, 256 devices: a whole 4x4x8 slice. The times are simulated.
256 devices in a mesh: shard: 32 (over y, z), rep: 8 (over x, core).
Axes of the slice: x: 4, y: 4, z: 8, core: 2. Of those that a mesh axis runs over, the one named last changes fastest.
Arguments:
- pooled_grad: float32 [65536, 32, 256], P(('rep', 'shard')), may hold values from -0.24 to 0.24
- present_count: int32 [256, 32], P(('rep', 'shard')), may hold values from 64 to 256, as said below
- members: int32 [65536, 32, 8], P('rep', 'shard'), may hold values from 0 to 511
- rep_pos: int32 [8, 32, 512], P('rep', 'shard'), may hold values from 0 to 1023, as said below
- row_ids: int32 [32, 1024], P('shard'), may hold values from 0 to 4095, as said below
- table: float32 [32, 4096, 256], P('shard'), may hold values from -6 to 6
- accum: float32 [32, 4096], P('shard'), may hold values from 0.5 to 20
Outputs:
- new_rows: float32 [32, 1024, 256], P('shard')
- new_accum: float32 [32, 1024], P('shard')
Inputs may be any that keep to these rules, and one draw needn't show every extreme that they name: Every row of present_count has the value 256 in some column. `rep_pos`: for each replica group and table the 512 places are distinct. `row_ids`: for each table the 1024 ids are distinct.
All inputs are finite; a program needn't handle non-finite values. Where the computation divides by a largest or mean magnitude, that divisor is 1e-20 or more.
Results may differ from a plain program's by a relative error of at most 0.00105.
Values may be sent and summed in bfloat16 or wider, within the bound.
No kernel may reach another device: no remote copies, remote signals or barrier semaphores. Data moves between devices by JAX's collectives and lax.ppermute only.
A program may use at most 128 MiB of HBM per device.

v0:
```python
import jax
import jax.numpy as jnp
from jax import lax
from jax.sharding import PartitionSpec as P

LEARN_RATE = 0.5
SCALE_EPS = 1e-06
ADAGRAD_EPS = 1e-08


def adagrad(summed, row_index, table_rows, state_rows):
    old_rows = jnp.take(table_rows, row_index, axis=0)
    old_state = jnp.take(state_rows, row_index, axis=0)
    new_state = old_state + jnp.mean(summed * summed, axis=1)
    updated = old_rows - LEARN_RATE * summed / (jnp.sqrt(new_state)[:, None] + ADAGRAD_EPS)
    return (updated, new_state)


def local(pooled_grad, present_count, members, rep_pos, row_ids, table, accum):
    b_local = pooled_grad.shape[0]
    position = lax.broadcasted_iota(jnp.int32, (b_local, pooled_grad.shape[1]), 0)
    present = (position < present_count[0][None, :]).astype(jnp.float32)
    masked = pooled_grad * present[:, :, None]
    chosen = members[:, 0, :]
    touched = rep_pos.shape[2]
    slot_ids = lax.broadcasted_iota(jnp.int32, (chosen.shape[0], touched), 1)
    counts = jnp.zeros((chosen.shape[0], touched), jnp.float32)
    for slot in range(chosen.shape[1]):
        counts = counts + (chosen[:, slot : slot + 1] == slot_ids).astype(jnp.float32)
    arrived = lax.all_to_all(masked, "shard", split_axis=1, concat_axis=0, tiled=True)
    row_grads = lax.dot_general(
        counts,
        arrived[:, 0, :],
        (((0,), (0,)), ((), ())),
        precision=lax.Precision.HIGHEST,
        preferred_element_type=jnp.float32,
    )
    row_scale = jnp.max(jnp.abs(row_grads), axis=1) + SCALE_EPS
    quantized = (row_grads / row_scale[:, None]).astype(jnp.bfloat16)
    active = row_ids.shape[1]
    placement = (
        lax.broadcasted_iota(jnp.int32, (active, touched), 0) == rep_pos[0, 0][None, :]
    ).astype(jnp.float32)
    dense_quant = jnp.dot(
        placement,
        quantized.astype(jnp.float32),
        precision=lax.Precision.HIGHEST,
        preferred_element_type=jnp.float32,
    ).astype(jnp.bfloat16)
    dense_scale = jnp.dot(
        placement, row_scale, precision=lax.Precision.HIGHEST, preferred_element_type=jnp.float32
    )
    all_quant, all_scale = (
        lax.all_gather(dense_quant[None], "rep", axis=0, tiled=True),
        lax.all_gather(dense_scale[None].astype(jnp.bfloat16), "rep", axis=0, tiled=True).astype(
            jnp.float32
        ),
    )
    summed = jnp.sum(all_quant.astype(jnp.float32) * all_scale[:, :, None], axis=0)
    updated, new_state = adagrad(summed, row_ids[0], table[0], accum[0])
    return (updated[None], new_state[None])


def solution(mesh):
    in_specs = (
        P(("rep", "shard"), None, None),
        P(("rep", "shard"), None),
        P("rep", "shard", None),
        P("rep", "shard", None),
        P("shard", None),
        P("shard", None, None),
        P("shard", None),
    )
    out_specs = (P("shard", None, None), P("shard", None))
    return jax.shard_map(local, mesh=mesh, in_specs=in_specs, out_specs=out_specs, check_vma=False)
```

profile of v0, /device:TPU:1, one launch (start us, length us, event | category | flops | bytes accessed | tf_op | source)
XLA Modules:
  0.0 293.3 jit_solution(17040944760913506652)
XLA Ops:
  7.2 0.0 copy-start
  7.2 0.7 fusion.32
  7.9 0.0 copy-start.1
  7.9 10.8 %copy_multiply_fusion = f32[256,32,256]{2,0,1:T(8,128)} fusion(f32[256,32,256]{2,1,0:T(8,128)} %param.7, f32[256,32]{0,1:T(8,128)S(1)} %fusion.32), kind=kLoop, calls=%fused_computation.28 | loop fusion | flops 2097152 | bytes 16809984 | tf_op jit(solution)/shard_map/mul | solution.py:23
  18.7 12.2 %all-to-all-start = ((f32[256,32,256]{2,0,1:T(8,128)}), f32[256,32,256]{2,0,1:T(8,128)}, u32[]{:S(2)}, u32[]{:S(2)}) async-start(f32[256,32,256]{2,0,1:T(8,128)} %copy_multiply_fusion), calls=%async_computation | async-start | bytes 16777216 | tf_op jit(solution)/shard_map/all_to_all | solution.py:30
  30.8 0.2 all-gather.4.cloned.1.call-start
  31.1 0.0 copy-done.1
  31.1 0.2 fusion.34
  31.3 16.4 %fusion.1.clone.4 = f32[8192,512]{1,0:T(8,128)} fusion(s32[8192]{0:T(1024)S(1)} %bitcast.45, s32[8192]{0:T(1024)S(1)} %bitcast.46, s32[8192]{0:T(1024)S(1)} %bitcast.47, s32[8192]{0:T(1024)S(1)} %bitcast.48, s32[8192]{0:T(1024)S(1)} %bitcast.49, s32[8192]{0:T(1024)S(1)} %bitcast.50, s32[8192]{0:T(1024)S(1)} %bitcast.51, s32[8192]{0:T(1024)S(1)} %bitcast.44), kind=kLoop, calls=%fused_computation.3.clone.clone.clone.1 | loop fusion | flops 96468992 | bytes 17039360 | tf_op jit(solution)/shard_map/reduce_max | solution.py:38
  47.7 0.0 copy-start.3
  47.7 0.0 copy-start.2
  47.7 171.3 %all-to-all-done = f32[256,32,256]{2,0,1:T(8,128)} async-done(((f32[256,32,256]{2,0,1:T(8,128)}), f32[256,32,256]{2,0,1:T(8,128)}, u32[]{:S(2)}, u32[]{:S(2)}) %all-to-all-start) | async-done | bytes 8388640 | tf_op jit(solution)/shard_map/all_to_all | solution.py:30
  219.0 19.4 %abs_reduce_fusion = (f32[512]{0:T(512)S(1)}, f32[512,256]{0,1:T(8,128)S(1)}) fusion(f32[8192,256]{1,0:T(8,128)} %bitcast.18, f32[8192,512]{1,0:T(8,128)} %fusion.1.clone.4), kind=kOutput, calls=%fused_computation.48 | convolution fusion | flops 12885164032 | bytes 25692160 | tf_op jit(solution)/shard_map/dot_general | solution.py:31
  238.5 0.0 copy-done.3
  238.5 1.3 fusion.27
  239.8 0.0 all-gather.4.cloned.1.call-update
  239.8 0.0 copy-done.2
  239.8 0.0 copy-done
  239.8 6.2 %gather_fusion.1 = f32[1024]{0:T(1024)S(1)} fusion(f32[4096]{0:T(1024)S(1)} %bitcast.40, s32[1024]{0:T(1024)S(1)} %broadcast_clamp_fusion), kind=kCustom, calls=%fused_computation.1 | custom fusion | bytes 12288 | tf_op jit(solution)/shard_map/jit(_take)/gather | solution.py:13
  246.0 5.7 %gather_fusion = f32[1024,256]{1,0:T(8,128)S(1)} fusion(f32[4096,256]{1,0:T(8,128)} %bitcast.41, s32[1024]{0:T(1024)S(1)} %broadcast_clamp_fusion), kind=kCustom, calls=%fused_computation | custom fusion | bytes 2101248 | tf_op jit(solution)/shard_map/jit(_take)/gather | solution.py:12
  251.7 1.0 fusion.25
  252.7 13.3 %all-gather.1 = bf16[8192]{0:T(1024)(128)(2,1)S(1)} all-gather(bf16[1024]{0:T(1024)(128)(2,1)S(1)} %convert_element_type.63), channel_id=3, replica_groups=mesh['shard'=32,'rep'=8] {'rep'}, dimensions={0}, use_global_device_ids=true | all-gather | bytes 18432 | tf_op jit(solution)/shard_map/all_gather | solution.py:55
  266.0 15.4 %all-gather.4.cloned.1.call-done = bf16[8192,256]{1,0:T(8,128)(2,1)} async-done(((bf16[1024,256]{1,0:T(8,128)(2,1)}), bf16[8192,256]{1,0:T(8,128)(2,1)}) %all-gather.4.cloned.1.call-update) | async-done | bytes 4194320 | tf_op jit(solution)/shard_map/all_gather | solution.py:54
  281.4 2.9 fusion.16
  284.3 0.2 multiply_reduce_fusion
  284.5 0.6 fusion.33
  285.1 1.3 fusion.28
  (6 shorter events, 0.0 us)
Async XLA Ops:
  7.2 232.7 %copy-start = (f32[1,4096]{1,0:T(1,128)S(1)}, f32[1,4096]{1,0:T(1,128)}, u32[]{:S(2)}) copy-start(f32[1,4096]{1,0:T(1,128)} %param.13) | copy-start | bytes 49156
  7.9 23.2 %copy-start.1 = (s32[8192,1,8]{0,2,1:T(8,128)S(1)}, s32[8192,1,8]{0,2,1:T(8,128)}, u32[]{:S(2)}) copy-start(s32[8192,1,8]{0,2,1:T(8,128)} %param.9) | copy-start | bytes 786436
  18.7 200.4 %all-to-all-start = ((f32[256,32,256]{2,0,1:T(8,128)}), f32[256,32,256]{2,0,1:T(8,128)}, u32[]{:S(2)}, u32[]{:S(2)}) async-start(f32[256,32,256]{2,0,1:T(8,128)} %copy_multiply_fusion), calls=%async_computation | async-start | bytes 16777216 | tf_op jit(solution)/shard_map/all_to_all | solution.py:30
  30.8 250.5 %all-gather.4.cloned.1.call-start = ((), (), s32[]{:S(2)}) async-start(), calls=%async_computation.1 | async-start | bytes 4718592 | tf_op jit(solution)/shard_map/all_gather | solution.py:54
  47.7 190.8 %copy-start.3 = (s32[1,1,512]{2,1,0:T(1,128)S(1)}, s32[1,1,512]{2,1,0:T(1,128)}, u32[]{:S(2)}) copy-start(s32[1,1,512]{2,1,0:T(1,128)} %param.10) | copy-start | bytes 6148
  47.7 192.1 %copy-start.2 = (s32[1,1024]{1,0:T(1,128)S(1)}, s32[1,1024]{1,0:T(1,128)}, u32[]{:S(2)}) copy-start(s32[1,1024]{1,0:T(1,128)} %param.11) | copy-start | bytes 12292
Sparse Core Ops, SparseCore 0:
  239.9 41.3 all-gather.3
where the time goes:
time: 294 us; the launch traced here: 293 us
  waiting for transfers between devices  187 us (64%)
  other arithmetic  33 us (11%)
  matrix products  21.7 us (7%)
  between operations  14.2 us (5%)
  blocking collectives  13.3 us (5%)
  starting transfers between devices  12.4 us (4%)
  local copies, waits for them, and re-layouts  12 us (4%)
    all_to_all x1, waiting for transfers between devices, local(): lax.all_to_all(masked, 'shard', split_axis=1, concat_axis=0, tiled=True)  171 us
    dot_general x1, matrix products, local(): lax.dot_general(counts, arrived[:, 0, :], (((0,), (0,)), ((), ())), preci...  19.4 us
    reduce_max x1, other arithmetic, local(): row_scale = jnp.max(jnp.abs(row_grads), axis=1) + SCALE_EPS  16.4 us
    all_gather x1, waiting for transfers between devices, local(): lax.all_gather(dense_quant[None], 'rep', axis=0, tiled=True)  15.4 us
    all_gather x1, blocking collectives, local(): lax.all_gather(dense_scale[None].astype(jnp.bfloat16), 'rep', axis=0, til...  13.3 us
    all_to_all x1, starting transfers between devices, local(): lax.all_to_all(masked, 'shard', split_axis=1, concat_axis=0, tiled=True)  12.2 us
    mul x1, other arithmetic, local(): masked = pooled_grad * present[:, :, None]  10.8 us
    gather x1, local copies, waits for them, and re-layouts, adagrad(): old_state = jnp.take(state_rows, row_index, axis=0)  6.15 us
  transfers between devices with their start and end apart: 2, of which 2 were waited for; matrix products, arithmetic and copies ran while one was open for 10% of the time, Pallas kernels for 0%

commit v1 on v0

v1 whole, which is shorter than its diff:
```python
import functools

import jax
import jax.numpy as jnp
from jax import lax
from jax.experimental import pallas as pl
from jax.experimental.pallas import tpu as pltpu
from jax.sharding import Mesh
from jax.sharding import PartitionSpec as P

LEARN_RATE = 0.5
ADAGRAD_EPS = 1e-08
PLANE = ("y", "x", "core")
REP = ("x", "core")
MIB = 1 << 20


def mask_kernel(samples, count_ref, left_ref, right_ref, out_ref):
    tables = out_ref.shape[0]
    first = pl.program_id(0) * samples
    position = lax.broadcasted_iota(jnp.int32, (samples, 128), 0) + first
    for table in range(tables):
        present = position < count_ref[0, table]
        for side, grad_ref in enumerate((left_ref, right_ref)):
            rows = grad_ref[pl.ds(table, samples, stride=tables), :]
            kept = jnp.where(present, rows, 0.0)
            out_ref[table, :, pl.ds(side * 128, 128)] = kept.astype(jnp.bfloat16)


def masked_by_table(pooled_grad, present_count):
    batch, tables, width = pooled_grad.shape
    samples = 32
    rows = pooled_grad.reshape(batch * tables, width)
    return pl.pallas_call(
        functools.partial(mask_kernel, samples),
        grid=(batch // samples,),
        out_shape=jax.ShapeDtypeStruct((tables, batch, width), jnp.bfloat16),
        in_specs=[
            pl.BlockSpec(memory_space=pltpu.SMEM),
            pl.BlockSpec((samples * tables, 128), lambda i: (i, 0)),
            pl.BlockSpec((samples * tables, 128), lambda i: (i, 1)),
        ],
        out_specs=pl.BlockSpec((tables, samples, width), lambda i: (0, i, 0)),
        compiler_params=pltpu.CompilerParams(vmem_limit_bytes=16 * MIB),
        cost_estimate=pl.CostEstimate(flops=batch * tables * width, bytes_accessed=batch * tables * width * 6, transcendentals=0),
        name="mask",
    )(present_count, rows, rows)


def place_kernel(members_ref, pos_ref, out_ref):
    n_z, slots, wide = out_ref.shape
    n_y = members_ref.shape[1] // (n_z * 256)
    parts = [jnp.broadcast_to(pos_ref[:, pl.ds(128 * k, 128)], (slots, 128)) for k in range(4)]
    for y in range(n_y):
        for z in range(n_z):
            for half in range(2):
                member = members_ref[:, pl.ds((y * n_z + z) * 256 + half * 128, 128)]
                low, high = member & 127, member >> 7
                found = jnp.take_along_axis(parts[0], low, axis=1)
                for k in range(1, 4):
                    found = jnp.where(high == k, jnp.take_along_axis(parts[k], low, axis=1), found)
                out_ref[z, :, pl.ds(y * 256 + half * 128, 128)] = found


def places_of(members, rep_pos, n_z):
    batch, slots = members.shape
    return pl.pallas_call(
        place_kernel,
        out_shape=jax.ShapeDtypeStruct((n_z, slots, batch // n_z), jnp.int32),
        compiler_params=pltpu.CompilerParams(vmem_limit_bytes=16 * MIB),
        cost_estimate=pl.CostEstimate(flops=batch * slots * 8, bytes_accessed=batch * slots * 8, transcendentals=0),
        name="places",
    )(members.T, rep_pos)


def count_kernel(place_ref, out_ref):
    slots, samples = place_ref.shape[1:]
    place = place_ref[0].astype(jnp.int32)
    high, low = place >> 5, place & 31
    row = lax.broadcasted_iota(jnp.int32, (32, samples), 0).astype(jnp.bfloat16)
    for block in range(out_ref.shape[0] // 32):
        wanted = jnp.where(high == block, low, -1).astype(jnp.bfloat16)
        total = jnp.zeros((32, samples), jnp.bfloat16)
        for slot in range(slots):
            here = jnp.broadcast_to(wanted[slot : slot + 1], (32, samples)) == row
            total = total + jnp.where(here, jnp.bfloat16(1), jnp.bfloat16(0))
        out_ref[pl.ds(block * 32, 32), :] = total


def counts_of(places, active):
    reps, slots, wide = places.shape
    n_y = wide // 256
    return pl.pallas_call(
        count_kernel,
        grid=(n_y, reps),
        out_shape=jax.ShapeDtypeStruct((active, n_y * reps * 256), jnp.bfloat16),
        in_specs=[pl.BlockSpec((1, slots, 256), lambda y, r: (r, 0, y))],
        out_specs=pl.BlockSpec((active, 256), lambda y, r: (0, y * reps + r)),
        compiler_params=pltpu.CompilerParams(vmem_limit_bytes=16 * MIB),
        cost_estimate=pl.CostEstimate(flops=active * wide * reps * slots * 3, bytes_accessed=active * wide * reps * 2, transcendentals=0),
        name="counts",
    )(places)


def local(n_z, n_rep, pooled_grad, present_count, members, rep_pos, row_ids, table, accum):
    active, width = row_ids.shape[1], pooled_grad.shape[2]
    swap = [(z * n_rep + q, q * n_z + z) for z in range(n_z) for q in range(n_rep)]

    places = places_of(members[:, 0, :], rep_pos[0], n_z).astype(jnp.int16)
    places = lax.ppermute(places, ("z",) + REP, swap)
    places = lax.all_to_all(places, "z", split_axis=0, concat_axis=0, tiled=True)
    counts = counts_of(places.astype(jnp.int32), active)

    masked = masked_by_table(pooled_grad, present_count)
    arrived = lax.all_to_all(masked, PLANE, split_axis=0, concat_axis=0, tiled=True)
    partial = jnp.dot(counts, arrived.reshape(-1, width), preferred_element_type=jnp.float32)

    chunks = partial.astype(jnp.bfloat16).reshape(n_z, active // n_z, width)
    chunks = lax.all_to_all(chunks, "z", split_axis=0, concat_axis=0, tiled=True)
    part = jnp.sum(chunks.astype(jnp.float32), axis=0).astype(jnp.bfloat16)
    part = lax.ppermute(part, ("z",) + REP, swap)
    summed = lax.all_gather(part, REP, axis=0, tiled=True).astype(jnp.float32)

    old_rows = jnp.take(table[0], row_ids[0], axis=0)
    old_state = jnp.take(accum[0], row_ids[0], axis=0)
    new_state = old_state + jnp.mean(summed * summed, axis=1)
    updated = old_rows - LEARN_RATE * summed / (jnp.sqrt(new_state)[:, None] + ADAGRAD_EPS)
    return (updated[None], new_state[None])


def solution(mesh):
    n_y, n_z, n_x, n_core = 4, 8, 4, 2
    grid = Mesh(mesh.devices.reshape(n_y, n_z, n_x, n_core), ("y", "z", "x", "core"))
    shard = ("y", "z")
    in_specs = (
        P(REP + shard, None, None),
        P(REP + shard, None),
        P(REP, shard, None),
        P(REP, shard, None),
        P(shard, None),
        P(shard, None, None),
        P(shard, None),
    )
    out_specs = (P(shard, None, None), P(shard, None))
    return jax.shard_map(
        functools.partial(local, n_z, n_x * n_core),
        mesh=grid,
        in_specs=in_specs,
        out_specs=out_specs,
        check_vma=False,
    )
```

time: 294 us -> 166 us (0.56)
  waiting for transfers between devices: 187 us -> 41 us
  other arithmetic: 33 us -> 2.28 us
  starting transfers between devices: 12.4 us -> 42.5 us
  Pallas kernels: 0 us -> 27.6 us
  between operations: 14.2 us -> 0.8 us
  local copies, waits for them, and re-layouts: 12 us -> 25.2 us
  matrix products: 21.7 us -> 12.2 us
    all_to_all x1 -> x3, waiting for transfers between devices: 171 us -> 38.3 us  [the longest x1 24.5 us: local(): lax.all_to_all(masked, PLANE, split_axis=0, concat_axis=0, tiled=True)]
    pallas_call x0 -> x3, Pallas kernels: none -> 27.6 us  [the longest x1 20 us: counts_of(): pl.pallas_call(count_kernel, grid=(n_y, reps), out_shape=jax.ShapeDtypeSt...]
    all_to_all x1 -> x3, starting transfers between devices: 12.2 us -> 30.9 us  [the longest x1 15.4 us: local(): lax.all_to_all(places, 'z', split_axis=0, concat_axis=0, tiled=True)]
    reduce_max x1 -> x0, other arithmetic: 16.4 us -> none  [local(): row_scale = jnp.max(jnp.abs(row_grads), axis=1) + SCALE_EPS]
    all_gather x1 -> x0, waiting for transfers between devices: 15.4 us -> none  [local(): lax.all_gather(dense_quant[None], 'rep', axis=0, tiled=True)]
    unnamed x8 -> x16, local copies, waits for them, and re-layouts: 0.02 us -> 13.4 us
    ppermute x0 -> x2, starting transfers between devices: none -> 11.6 us  [the longest x1 6.68 us: local(): part = lax.ppermute(part, ('z',) + REP, swap)]
    mul x1 -> x0, other arithmetic: 10.8 us -> none  [local(): masked = pooled_grad * present[:, :, None]]
  transfers between devices with their start and end apart: 2 -> 5, of which waited for: 2 -> 3; matrix products, arithmetic and copies ran while one was open for 10% -> 7% of each run, Pallas kernels for 0% -> 16%
where the time goes in v1:
time: 166 us; the launch traced here: 165 us
  starting transfers between devices  42.5 us (26%)
  waiting for transfers between devices  41 us (25%)
  Pallas kernels  27.6 us (17%)
  local copies, waits for them, and re-layouts  25.2 us (15%)
  blocking collectives  13.6 us (8%)
  matrix products  12.2 us (7%)
  other arithmetic  2.28 us (1%)
    all_to_all x1, waiting for transfers between devices, local(): lax.all_to_all(masked, PLANE, split_axis=0, concat_axis=0, tiled=True)  24.5 us
    pallas_call x1, Pallas kernels, counts_of(): pl.pallas_call(count_kernel, grid=(n_y, reps), out_shape=jax.ShapeDtypeSt...  20 us
    all_to_all x1, starting transfers between devices, local(): lax.all_to_all(places, 'z', split_axis=0, concat_axis=0, tiled=True)  15.4 us
    all_to_all x1, waiting for transfers between devices, local(): lax.all_to_all(chunks, 'z', split_axis=0, concat_axis=0, tiled=True)  13.8 us
    all_gather x1, blocking collectives, local(): summed = lax.all_gather(part, REP, axis=0, tiled=True).astype(jnp.float32)  13.6 us
    unnamed x16, local copies, waits for them, and re-layouts  13.4 us
    dot_general x1, matrix products, local(): jnp.dot(counts, arrived.reshape(-1, width), preferred_element_type=jnp.fl...  12.2 us
    all_to_all x1, starting transfers between devices, local(): lax.all_to_all(masked, PLANE, split_axis=0, concat_axis=0, tiled=True)  8.51 us
  transfers between devices with their start and end apart: 5, of which 3 were waited for; matrix products, arithmetic and copies ran while one was open for 7% of the time, Pallas kernels for 16%

profile of v1, /device:TPU:1, one launch (start us, length us, event | category | flops | bytes accessed | tf_op | source)
XLA Modules:
  0.0 165.2 jit_solution(5737696171996066460)
XLA Ops:
  0.6 0.0 copy-start
  0.6 0.0 copy-start.4
  0.7 0.9 copy-done.4
  1.6 0.7 copy-done.5
  2.3 0.5 places.1
  2.9 4.9 %collective-permute-start = (s16[8,8,1024]{2,1,0:T(8,128)(2,1)S(1)}, s16[8,8,1024]{2,1,0:T(8,128)(2,1)}, u32[]{:S(2)}, u32[]{:S(2)}) collective-permute-start(s16[8,8,1024]{2,1,0:T(8,128)(2,1)S(1)} %convert_element_type.14), channel_id=1, source_target_pairs={{0,0},{1,8},{2,16},{3,24},{4,32},{5,40},{6,48},{7,56},{8,1},{9,9},... | collective-permute-start | bytes 393224 | tf_op jit(solution)/shard_map/ppermute | solution.py:110
  7.8 2.7 %collective-permute-done = s16[8,8,1024]{2,1,0:T(8,128)(2,1)} collective-permute-done((s16[8,8,1024]{2,1,0:T(8,128)(2,1)S(1)}, s16[8,8,1024]{2,1,0:T(8,128)(2,1)}, u32[]{:S(2)}, u32[]{:S(2)}) %collective-permute-start) | collective-permute-done | bytes 131104 | tf_op jit(solution)/shard_map/ppermute | solution.py:110
  10.5 15.4 %all-to-all-start = ((s16[8,8,1024]{2,1,0:T(8,128)(2,1)}), s16[8,8,1024]{2,1,0:T(8,128)(2,1)S(1)}, u32[]{:S(2)}, u32[]{:S(2)}) async-start(s16[8,8,1024]{2,1,0:T(8,128)(2,1)} %collective-permute-done), calls=%async_computation | async-start | bytes 262144 | tf_op jit(solution)/shard_map/all_to_all | solution.py:111
  26.0 3.4 %copy-done.1 = f32[256,32,256]{2,1,0:T(8,128)S(1)} copy-done((f32[256,32,256]{2,1,0:T(8,128)S(1)}, f32[256,32,256]{2,1,0:T(8,128)}, u32[]{:S(2)}) %copy-start.1) | copy-done | bytes 8388632
  29.3 0.7 copy-done.6
  30.0 7.1 %mask.1 = bf16[32,256,256]{2,1,0:T(8,128)(2,1)S(1)} custom-call(s32[1,32]{1,0:T(1,128)S(1)} %copy-done.6, f32[8192,256]{1,0:T(8,128)S(1)} %bitcast.20, f32[8192,256]{1,0:T(8,128)S(1)} %bitcast.21), custom_call_target="tpu_custom_call" | custom-call | flops 2097152 | bytes 12582912 | tf_op jit(solution)/shard_map/mask/pallas_call | solution.py:34
  37.1 0.0 copy-start.3
  37.1 1.9 %copy-done.3 = bf16[32,256,256]{2,1,0:T(8,128)(2,1)} copy-done((bf16[32,256,256]{2,1,0:T(8,128)(2,1)}, bf16[32,256,256]{2,1,0:T(8,128)(2,1)S(1)}, u32[]{:S(2)}) %copy-start.3) | copy-done | bytes 4194328
  39.0 0.0 all-to-all-done
  39.0 8.5 %all-to-all-start.1 = ((bf16[32,256,256]{2,1,0:T(8,128)(2,1)}), bf16[32,256,256]{2,1,0:T(8,128)(2,1)}, u32[]{:S(2)}, u32[]{:S(2)}) async-start(bf16[32,256,256]{2,1,0:T(8,128)(2,1)} %copy-done.3), calls=%async_computation.1 | async-start | bytes 8388608 | tf_op jit(solution)/shard_map/all_to_all | solution.py:115
  47.6 20.0 %counts.1 = bf16[1024,8192]{1,0:T(8,128)(2,1)S(1)} custom-call(s32[8,8,1024]{2,1,0:T(8,128)S(1)} %convert_element_type.15.place_ref), custom_call_target="tpu_custom_call" | custom-call | flops 201326592 | bytes 16777216 | tf_op jit(solution)/shard_map/counts/pallas_call | solution.py:93
  67.6 0.0 copy-start.2
  67.6 5.7 %copy-done.2 = bf16[1024,8192]{1,0:T(8,128)(2,1)} copy-done((bf16[1024,8192]{1,0:T(8,128)(2,1)}, bf16[1024,8192]{1,0:T(8,128)(2,1)S(1)}, u32[]{:S(2)}) %copy-start.2) | copy-done | bytes 16777240
  73.3 24.5 %all-to-all-done.1 = bf16[32,256,256]{2,1,0:T(8,128)(2,1)} async-done(((bf16[32,256,256]{2,1,0:T(8,128)(2,1)}), bf16[32,256,256]{2,1,0:T(8,128)(2,1)}, u32[]{:S(2)}, u32[]{:S(2)}) %all-to-all-start.1) | async-done | bytes 4194336 | tf_op jit(solution)/shard_map/all_to_all | solution.py:115
  97.8 12.2 %convolution_convert_fusion = bf16[1024,256]{1,0:T(8,128)(2,1)} fusion(bf16[1024,8192]{1,0:T(8,128)(2,1)} %copy-done.2, bf16[8192,256]{1,0:T(8,128)(2,1)} %bitcast.8), kind=kOutput, calls=%fused_computation.4 | convolution fusion | flops 4295229440 | bytes 21495808 | tf_op jit(solution)/shard_map/dot_general | solution.py:116
  110.1 6.9 %all-to-all-start.2 = ((bf16[8,128,256]{2,1,0:T(8,128)(2,1)}), bf16[8,128,256]{2,1,0:T(8,128)(2,1)S(1)}, u32[]{:S(2)}, u32[]{:S(2)}) async-start(bf16[8,128,256]{2,1,0:T(8,128)(2,1)} %bitcast.9), calls=%async_computation.2 | async-start | bytes 1048576 | tf_op jit(solution)/shard_map/all_to_all | solution.py:119
  117.0 0.0 copy-done.7
  117.0 13.8 %all-to-all-done.2 = bf16[8,128,256]{2,1,0:T(8,128)(2,1)S(1)} async-done(((bf16[8,128,256]{2,1,0:T(8,128)(2,1)}), bf16[8,128,256]{2,1,0:T(8,128)(2,1)S(1)}, u32[]{:S(2)}, u32[]{:S(2)}) %all-to-all-start.2) | async-done | bytes 524320 | tf_op jit(solution)/shard_map/all_to_all | solution.py:119
  130.8 0.1 reduce_sum.21
  130.9 6.7 %collective-permute-start.1 = (bf16[128,256]{1,0:T(8,128)(2,1)S(1)}, bf16[128,256]{1,0:T(8,128)(2,1)S(1)}, u32[]{:S(2)}, u32[]{:S(2)}) collective-permute-start(bf16[128,256]{1,0:T(8,128)(2,1)S(1)} %reduce_sum.21), channel_id=1, source_target_pairs={{0,0},{1,8},{2,16},{3,24},{4,32},{5,40},{6,48},{7,56},{8,1},{9,9},... | collective-permute-start | bytes 196616 | tf_op jit(solution)/shard_map/ppermute | solution.py:121
  137.6 6.2 %gather_fusion.1 = f32[1024]{0:T(1024)S(1)} fusion(f32[4096]{0:T(1024)S(1)} %bitcast.19, s32[1024]{0:T(1024)S(1)} %broadcast_clamp_fusion), kind=kCustom, calls=%fused_computation.1 | custom fusion | bytes 12288 | tf_op jit(solution)/shard_map/jit(_take)/gather | solution.py:125
  143.8 5.7 %gather_fusion = f32[1024,256]{1,0:T(8,128)S(1)} fusion(f32[4096,256]{1,0:T(8,128)} %bitcast.24, s32[1024]{0:T(1024)S(1)} %broadcast_clamp_fusion), kind=kCustom, calls=%fused_computation | custom fusion | bytes 2101248 | tf_op jit(solution)/shard_map/jit(_take)/gather | solution.py:124
  149.4 0.0 collective-permute-done.1
  149.4 13.6 %all_gather.3 = bf16[1024,256]{1,0:T(8,128)(2,1)S(1)} all-gather(bf16[128,256]{1,0:T(8,128)(2,1)S(1)} %collective-permute-done.1), channel_id=1, replica_groups=mesh['y'=4,'z'=8,'x'=4,'core'=2] {'x','core'}, dimensions={0}, use_global_device_ids=true | all-gather | bytes 589824 | tf_op jit(solution)/shard_map/all_gather | solution.py:122
  163.1 0.2 fusion.3
  163.3 0.6 fusion.4
  163.9 1.3 fusion.2
  (10 shorter events, 0.1 us)
Async XLA Ops:
  0.6 137.0 %copy-start = (f32[1,4096]{1,0:T(1,128)S(1)}, f32[1,4096]{1,0:T(1,128)}, u32[]{:S(2)}) copy-start(f32[1,4096]{1,0:T(1,128)} %param.13) | copy-start | bytes 49156
  0.6 1.0 copy-start.4
  1.6 0.7 copy-start.5
  2.9 7.7 %collective-permute-start = (s16[8,8,1024]{2,1,0:T(8,128)(2,1)S(1)}, s16[8,8,1024]{2,1,0:T(8,128)(2,1)}, u32[]{:S(2)}, u32[]{:S(2)}) collective-permute-start(s16[8,8,1024]{2,1,0:T(8,128)(2,1)S(1)} %convert_element_type.14), channel_id=1, source_target_pairs={{0,0},{1,8},{2,16},{3,24},{4,32},{5,40},{6,48},{7,56},{8,1},{9,9},... | collective-permute-start | bytes 393224 | tf_op jit(solution)/shard_map/ppermute | solution.py:110
  10.5 28.5 %all-to-all-start = ((s16[8,8,1024]{2,1,0:T(8,128)(2,1)}), s16[8,8,1024]{2,1,0:T(8,128)(2,1)S(1)}, u32[]{:S(2)}, u32[]{:S(2)}) async-start(s16[8,8,1024]{2,1,0:T(8,128)(2,1)} %collective-permute-done), calls=%async_computation | async-start | bytes 262144 | tf_op jit(solution)/shard_map/all_to_all | solution.py:111
  26.0 3.4 %copy-start.1 = (f32[256,32,256]{2,1,0:T(8,128)S(1)}, f32[256,32,256]{2,1,0:T(8,128)}, u32[]{:S(2)}) copy-start(f32[256,32,256]{2,1,0:T(8,128)} %param.7) | copy-start | bytes 25165828
  29.3 0.7 copy-start.6
  37.1 1.9 %copy-start.3 = (bf16[32,256,256]{2,1,0:T(8,128)(2,1)}, bf16[32,256,256]{2,1,0:T(8,128)(2,1)S(1)}, u32[]{:S(2)}) copy-start(bf16[32,256,256]{2,1,0:T(8,128)(2,1)S(1)} %mask.1) | copy-start | bytes 12582916
  39.0 58.8 %all-to-all-start.1 = ((bf16[32,256,256]{2,1,0:T(8,128)(2,1)}), bf16[32,256,256]{2,1,0:T(8,128)(2,1)}, u32[]{:S(2)}, u32[]{:S(2)}) async-start(bf16[32,256,256]{2,1,0:T(8,128)(2,1)} %copy-done.3), calls=%async_computation.1 | async-start | bytes 8388608 | tf_op jit(solution)/shard_map/all_to_all | solution.py:115
  67.6 5.7 %copy-start.2 = (bf16[1024,8192]{1,0:T(8,128)(2,1)}, bf16[1024,8192]{1,0:T(8,128)(2,1)S(1)}, u32[]{:S(2)}) copy-start(bf16[1024,8192]{1,0:T(8,128)(2,1)S(1)} %counts.1) | copy-start | bytes 50331652
  97.8 19.2 %copy-start.7 = (s32[1,1024]{1,0:T(1,128)S(1)}, s32[1,1024]{1,0:T(1,128)}, u32[]{:S(2)}) copy-start(s32[1,1024]{1,0:T(1,128)} %param.11) | copy-start | bytes 12292
  110.1 20.8 %all-to-all-start.2 = ((bf16[8,128,256]{2,1,0:T(8,128)(2,1)}), bf16[8,128,256]{2,1,0:T(8,128)(2,1)S(1)}, u32[]{:S(2)}, u32[]{:S(2)}) async-start(bf16[8,128,256]{2,1,0:T(8,128)(2,1)} %bitcast.9), calls=%async_computation.2 | async-start | bytes 1048576 | tf_op jit(solution)/shard_map/all_to_all | solution.py:119
  130.9 18.5 %collective-permute-start.1 = (bf16[128,256]{1,0:T(8,128)(2,1)S(1)}, bf16[128,256]{1,0:T(8,128)(2,1)S(1)}, u32[]{:S(2)}, u32[]{:S(2)}) collective-permute-start(bf16[128,256]{1,0:T(8,128)(2,1)S(1)} %reduce_sum.21), channel_id=1, source_target_pairs={{0,0},{1,8},{2,16},{3,24},{4,32},{5,40},{6,48},{7,56},{8,1},{9,9},... | collective-permute-start | bytes 196616 | tf_op jit(solution)/shard_map/ppermute | solution.py:121

commit v2 on v1

v2 whole, which is shorter than its diff:
```python
import functools

import jax
import jax.numpy as jnp
from jax import lax
from jax.experimental import pallas as pl
from jax.experimental.pallas import tpu as pltpu
from jax.sharding import Mesh
from jax.sharding import PartitionSpec as P

LEARN_RATE = 0.5
ADAGRAD_EPS = 1e-08
REP = ("x", "core")
MIB = 1 << 20


def mask_kernel(n_z, count_ref, grad_ref, out_ref):
    tables, samples, width = out_ref.shape
    n_y = tables // n_z
    first = pl.program_id(0) * samples
    to = lax.broadcasted_iota(jnp.int32, (256, 256), 0)
    source = lax.broadcasted_iota(jnp.int32, (256, 256), 1)
    permute = ((source % 16) * 16 + source // 16 == to).astype(jnp.bfloat16)
    position = lax.broadcasted_iota(jnp.int32, (16, width), 0) + first
    for sample in range(0, samples, 16):
        for table in range(0, tables, 16):
            rows = grad_ref[sample : sample + 16, table : table + 16, :].reshape(256, width)
            moved = jnp.dot(permute, rows.astype(jnp.bfloat16), preferred_element_type=jnp.float32)
            for j in range(16):
                present = position + sample < count_ref[0, table + j]
                kept = jnp.where(present, moved[j * 16 : j * 16 + 16], 0.0)
                place = (table + j) % n_z * n_y + (table + j) // n_z
                out_ref[place, sample : sample + 16, :] = kept.astype(jnp.bfloat16)


def masked_by_table(n_z, pooled_grad, present_count):
    batch, tables, width = pooled_grad.shape
    samples = 128
    return pl.pallas_call(
        functools.partial(mask_kernel, n_z),
        grid=(batch // samples,),
        out_shape=jax.ShapeDtypeStruct((tables, batch, width), jnp.bfloat16),
        in_specs=[
            pl.BlockSpec(memory_space=pltpu.SMEM),
            pl.BlockSpec((samples, tables, width), lambda i: (i, 0, 0)),
        ],
        out_specs=pl.BlockSpec((tables, samples, width), lambda i: (0, i, 0)),
        compiler_params=pltpu.CompilerParams(vmem_limit_bytes=56 * MIB),
        cost_estimate=pl.CostEstimate(flops=batch * tables * width, bytes_accessed=batch * tables * width * 6, transcendentals=0),
        name="mask",
    )(present_count, pooled_grad)


def lists_kernel(members_ref, pos_ref, out_ref):
    n_z, wide = out_ref.shape[0] - 1, out_ref.shape[2]
    n_y, touched = wide // 256, pos_ref.shape[1]
    for y in range(n_y):
        for z in range(n_z):
            out_ref[z, :, pl.ds(y * 256, 256)] = members_ref[:, pl.ds((y * n_z + z) * 256, 256)]
    out_ref[n_z] = jnp.zeros(out_ref.shape[1:], jnp.int32)
    out_ref[n_z, pl.ds(0, 1), pl.ds(0, touched)] = pos_ref[...]


def lists_of(members, rep_pos, n_z):
    batch, slots = members.shape
    return pl.pallas_call(
        lists_kernel,
        out_shape=jax.ShapeDtypeStruct((n_z + 1, slots, batch // n_z), jnp.int32),
        compiler_params=pltpu.CompilerParams(vmem_limit_bytes=8 * MIB),
        cost_estimate=pl.CostEstimate(flops=batch * slots, bytes_accessed=batch * slots * 8, transcendentals=0),
        name="lists",
    )(members.T, rep_pos)


def one_hot_rows(values, row):
    return jnp.where(jnp.broadcast_to(values, row.shape) == row, jnp.bfloat16(1), jnp.bfloat16(0))


def count_kernel(member_ref, out_ref):
    slots, samples = member_ref.shape[1:]
    rows = 32
    base = lax.broadcasted_iota(jnp.int32, (rows, 128), 0).astype(jnp.bfloat16)

    def lanes(i, carry):
        at = pl.ds(pl.multiple_of(i * 128, 128), 128)
        member = member_ref[0, :, at]
        high, low = member >> 8, member & 255
        for block in range(out_ref.shape[1] // 256):
            wanted = jnp.where(high == block, low, -1).astype(jnp.bfloat16)
            for first in range(0, 256, rows):
                row = base + jnp.bfloat16(first)
                total = one_hot_rows(wanted[0:1], row)
                for s in range(1, slots):
                    total = total + one_hot_rows(wanted[s : s + 1], row)
                out_ref[0, pl.ds(block * 256 + first, rows), at] = total
        return carry

    lax.fori_loop(0, samples // 128, lanes, 0)


def counts_of(members, touched):
    reps, slots, wide = members.shape
    return pl.pallas_call(
        count_kernel,
        grid=(reps,),
        in_specs=[pl.BlockSpec((1, slots, wide), lambda r: (r, 0, 0))],
        out_specs=pl.BlockSpec((1, touched, wide), lambda r: (r, 0, 0)),
        out_shape=jax.ShapeDtypeStruct((reps, touched, wide), jnp.bfloat16),
        compiler_params=pltpu.CompilerParams(vmem_limit_bytes=56 * MIB),
        cost_estimate=pl.CostEstimate(flops=touched * wide * reps * slots * 3, bytes_accessed=touched * wide * reps * 2, transcendentals=0),
        name="counts",
    )(members)


AHEAD = 3


def plane_kernel(count_hbm, bags_hbm, pos_ref, out_ref, count_buf, bags_buf, place_buf, grad_buf, total_ref, count_sem, bags_sem):
    reps, touched, samples = count_hbm.shape
    active = out_ref.shape[0]
    row = lax.broadcasted_iota(jnp.int32, (256, 128), 0).astype(jnp.bfloat16)

    def copies(rep):
        slot = rep % AHEAD
        bags = bags_hbm.at[pl.ds(rep * samples, samples), :]
        return (
            pltpu.make_async_copy(count_hbm.at[rep], count_buf.at[slot], count_sem.at[slot]),
            pltpu.make_async_copy(bags, bags_buf.at[slot], bags_sem.at[slot]),
        )

    for rep in range(AHEAD - 1):
        for copy in copies(rep):
            copy.start()
    for rep in range(reps):
        if rep + AHEAD - 1 < reps:
            for copy in copies(rep + AHEAD - 1):
                copy.start()
        first = rep % 2 * touched
        for lane in range(0, touched, 128):
            pos = pos_ref[rep : rep + 1, lane : lane + 128]
            for block in range(active // 256):
                wanted = jnp.where((pos >> 8) == block, pos & 255, -1).astype(jnp.bfloat16)
                place_buf[pl.ds(block * 256, 256), pl.ds(first + lane, 128)] = one_hot_rows(wanted, row)
        for copy in copies(rep):
            copy.wait()
        slot = rep % AHEAD
        grads = jnp.dot(count_buf[slot], bags_buf[slot], preferred_element_type=jnp.float32)
        grad_buf[pl.ds(first, touched), :] = grads.astype(jnp.bfloat16)
        if rep % 2:
            sums = jnp.dot(place_buf[...], grad_buf[...], preferred_element_type=jnp.float32)
            if rep == 1:
                total_ref[...] = sums
            elif rep < reps - 1:
                total_ref[...] += sums
            else:
                out_ref[...] = (total_ref[...] + sums).astype(jnp.bfloat16)


def plane_sum(counts, bags, pos, active):
    reps, touched, samples = counts.shape
    width = bags.shape[1]
    return pl.pallas_call(
        plane_kernel,
        out_shape=jax.ShapeDtypeStruct((active, width), jnp.bfloat16),
        in_specs=[
            pl.BlockSpec(memory_space=pl.ANY),
            pl.BlockSpec(memory_space=pl.ANY),
            pl.BlockSpec(memory_space=pltpu.VMEM),
        ],
        out_specs=pl.BlockSpec(memory_space=pltpu.VMEM),
        scratch_shapes=[
            pltpu.VMEM((AHEAD, touched, samples), jnp.bfloat16),
            pltpu.VMEM((AHEAD, samples, width), jnp.bfloat16),
            pltpu.VMEM((active, 2 * touched), jnp.bfloat16),
            pltpu.VMEM((2 * touched, width), jnp.bfloat16),
            pltpu.VMEM((active, width), jnp.float32),
            pltpu.SemaphoreType.DMA((AHEAD,)),
            pltpu.SemaphoreType.DMA((AHEAD,)),
        ],
        compiler_params=pltpu.CompilerParams(vmem_limit_bytes=56 * MIB),
        cost_estimate=pl.CostEstimate(
            flops=2 * reps * touched * (samples + active) * width,
            bytes_accessed=reps * samples * (touched + width) * 2,
            transcendentals=0,
        ),
        name="plane_sum",
    )(counts, bags, pos)


def local(n_z, n_rep, pooled_grad, present_count, members, rep_pos, row_ids, table, accum):
    active, width = row_ids.shape[1], pooled_grad.shape[2]
    swap = [(z * n_rep + q, q * n_z + z) for z in range(n_z) for q in range(n_rep)]

    lists = lists_of(members[:, 0, :], rep_pos[0], n_z).astype(jnp.int16)
    lists = lax.ppermute(lists, ("z",) + REP, swap)
    lists = lax.all_gather(lists, "z", axis=0, tiled=False)
    here = lax.dynamic_index_in_dim(lists, lax.axis_index("z"), 1, False).astype(jnp.int32)
    touched = rep_pos.shape[2]
    pos = lists[:, n_z, 0, :touched].astype(jnp.int32)

    masked = masked_by_table(n_z, pooled_grad, present_count)
    arrived = lax.all_to_all(masked, REP + ("y",), split_axis=0, concat_axis=0, tiled=True)

    counts = counts_of(here, touched)
    partial = plane_sum(counts, arrived.reshape(-1, width), pos, active)

    chunks = partial.reshape(n_z, active // n_z, width)
    chunks = lax.all_to_all(chunks, "z", split_axis=0, concat_axis=0, tiled=True)
    old_rows = jnp.take(table[0], row_ids[0], axis=0)
    old_state = jnp.take(accum[0], row_ids[0], axis=0)
    chunks, old_rows, old_state = lax.optimization_barrier((chunks, old_rows, old_state))
    part = jnp.sum(chunks.astype(jnp.float32), axis=0).astype(jnp.bfloat16)
    part = lax.ppermute(part, ("z",) + REP, swap)
    summed = lax.all_gather(part, REP, axis=0, tiled=True).astype(jnp.float32)

    new_state = old_state + jnp.mean(summed * summed, axis=1)
    updated = old_rows - LEARN_RATE * summed / (jnp.sqrt(new_state)[:, None] + ADAGRAD_EPS)
    return (updated[None], new_state[None])


def solution(mesh):
    n_y, n_z, n_x, n_core = 4, 8, 4, 2
    grid = Mesh(mesh.devices.reshape(n_y, n_z, n_x, n_core), ("y", "z", "x", "core"))
    shard = ("y", "z")
    in_specs = (
        P(REP + shard, None, None),
        P(REP + shard, None),
        P(REP, shard, None),
        P(REP, shard, None),
        P(shard, None),
        P(shard, None, None),
        P(shard, None),
    )
    out_specs = (P(shard, None, None), P(shard, None))
    return jax.shard_map(
        functools.partial(local, n_z, n_x * n_core),
        mesh=grid,
        in_specs=in_specs,
        out_specs=out_specs,
        check_vma=False,
    )
```

time: 166 us -> 141 us (0.85)
  blocking collectives: 13.6 us -> 53.7 us
  waiting for transfers between devices: 41 us -> 11.3 us
  local copies, waits for them, and re-layouts: 25.2 us -> 11.8 us
  matrix products: 12.2 us -> 0 us
  starting transfers between devices: 42.5 us -> 32 us
    all_gather x0 -> x1, blocking collectives: none -> 36.3 us  [local(): lists = lax.all_gather(lists, 'z', axis=0, tiled=False)]
    all_to_all x2 -> x1, waiting for transfers between devices: 24.5 us -> 0.01 us  [local(): lax.all_to_all(masked, REP + ('y',), split_axis=0, concat_axis=0, tiled=T...]
    all_to_all x2 -> x1, starting transfers between devices: 23.9 us -> 8.78 us  [local(): lax.all_to_all(masked, REP + ('y',), split_axis=0, concat_axis=0, tiled=T...]
    unnamed x16 -> x8, local copies, waits for them, and re-layouts: 13.4 us -> 0.02 us
    dot_general x1 -> x0, matrix products: 12.2 us -> none  [local(): jnp.dot(counts, arrived.reshape(-1, width), preferred_element_type=jnp.fl...]
    all_to_all x1, starting transfers between devices: 6.93 us -> 16.4 us  [local(): lax.all_to_all(chunks, 'z', split_axis=0, concat_axis=0, tiled=True)]
    all_to_all x1, waiting for transfers between devices: 13.8 us -> 5.38 us  [local(): lax.all_to_all(chunks, 'z', split_axis=0, concat_axis=0, tiled=True)]
    all_gather x1, blocking collectives: 13.6 us -> 17.5 us  [local(): summed = lax.all_gather(part, REP, axis=0, tiled=True).astype(jnp.float32)]
  transfers between devices with their start and end apart: 5 -> 4, of which waited for: 3 -> 3; matrix products, arithmetic and copies ran while one was open for 7% -> 10% of each run, Pallas kernels for 16% -> 7%
where the time goes in v2:
time: 141 us; the launch traced here: 140 us
  blocking collectives  53.7 us (38%)
  starting transfers between devices  32 us (23%)
  Pallas kernels  26.9 us (19%)
  local copies, waits for them, and re-layouts  11.8 us (8%)
  waiting for transfers between devices  11.3 us (8%)
  other arithmetic  3.65 us (3%)
    all_gather x1, blocking collectives, local(): lists = lax.all_gather(lists, 'z', axis=0, tiled=False)  36.3 us
    all_gather x1, blocking collectives, local(): summed = lax.all_gather(part, REP, axis=0, tiled=True).astype(jnp.float32)  17.5 us
    all_to_all x1, starting transfers between devices, local(): lax.all_to_all(chunks, 'z', split_axis=0, concat_axis=0, tiled=True)  16.4 us
    pallas_call x1, Pallas kernels, plane_sum(): pl.pallas_call(plane_kernel, out_shape=jax.ShapeDtypeStruct((active, widt...  11.5 us
    pallas_call x1, Pallas kernels, counts_of(): pl.pallas_call(count_kernel, grid=(reps,), in_specs=[pl.BlockSpec((1, slo...  9.7 us
    all_to_all x1, starting transfers between devices, local(): lax.all_to_all(masked, REP + ('y',), split_axis=0, concat_axis=0, tiled=T...  8.78 us
    gather x1, local copies, waits for them, and re-layouts, local(): old_state = jnp.take(accum[0], row_ids[0], axis=0)  6.15 us
    gather x1, local copies, waits for them, and re-layouts, local(): old_rows = jnp.take(table[0], row_ids[0], axis=0)  5.65 us
  transfers between devices with their start and end apart: 4, of which 3 were waited for; matrix products, arithmetic and copies ran while one was open for 10% of the time, Pallas kernels for 7%

profile of v2, /device:TPU:1, one launch (start us, length us, event | category | flops | bytes accessed | tf_op | source)
XLA Modules:
  0.0 140.1 jit_solution(4797036639786766314)
XLA Ops:
  0.6 0.0 copy-start
  0.6 5.6 %mask.1 = bf16[32,256,256]{2,1,0:T(8,128)(2,1)} custom-call(s32[1,32]{1,0:T(1,128)} %count_ref.1, f32[256,32,256]{2,1,0:T(8,128)} %grad_ref.1), custom_call_target="tpu_custom_call" | custom-call | flops 2097152 | bytes 12582912 | tf_op jit(solution)/shard_map/mask/pallas_call | solution.py:39
  6.3 0.0 copy-start.1
  6.3 0.0 copy-start.2
  6.3 8.8 %all-to-all-start = ((bf16[32,256,256]{2,1,0:T(8,128)(2,1)}), bf16[32,256,256]{2,1,0:T(8,128)(2,1)}, u32[]{:S(2)}, u32[]{:S(2)}) async-start(bf16[32,256,256]{2,1,0:T(8,128)(2,1)} %mask.1), calls=%async_computation | async-start | bytes 8388608 | tf_op jit(solution)/shard_map/all_to_all | solution.py:202
  15.0 0.0 copy-done.1
  15.1 0.0 copy-done.2
  15.1 3.7 %collective-permute-start = (s16[9,8,1024]{2,1,0:T(8,128)(2,1)S(1)}, s16[9,8,1024]{2,1,0:T(8,128)(2,1)S(1)}, u32[]{:S(2)}, u32[]{:S(2)}) collective-permute-start(s16[9,8,1024]{2,1,0:T(8,128)(2,1)S(1)} %convert_element_type.18), channel_id=1, source_target_pairs={{0,0},{1,8},{2,16},{3,24},{4,32},{5,40},{6,48},{7,56},{8,1},{9,9},... | collective-permute-start | bytes 442376 | tf_op jit(solution)/shard_map/ppermute | solution.py:195
  18.9 3.2 %collective-permute-done = s16[9,8,1024]{2,1,0:T(8,128)(2,1)S(1)} collective-permute-done((s16[9,8,1024]{2,1,0:T(8,128)(2,1)S(1)}, s16[9,8,1024]{2,1,0:T(8,128)(2,1)S(1)}, u32[]{:S(2)}, u32[]{:S(2)}) %collective-permute-start) | collective-permute-done | bytes 147488 | tf_op jit(solution)/shard_map/ppermute | solution.py:195
  22.1 36.3 %all-gather.2 = s16[72,8,1024]{2,1,0:T(8,128)(2,1)S(1)} all-gather(s16[9,8,1024]{2,1,0:T(8,128)(2,1)S(1)} %collective-permute-done), channel_id=2, replica_groups=mesh['y'=4,'z'=8,'x'=4,'core'=2] {'z'}, dimensions={0}, use_global_device_ids=true | all-gather | bytes 1327104 | tf_op jit(solution)/shard_map/all_gather | solution.py:196
  58.4 0.7 bitcast_convert_fusion.member_ref
  59.1 9.7 %counts.1.count_hbm = bf16[8,512,1024]{2,1,0:T(8,128)(2,1)} custom-call(s32[8,8,1024]{2,1,0:T(8,128)} %bitcast_convert_fusion.member_ref), custom_call_target="tpu_custom_call" | custom-call | flops 100663296 | bytes 8388608 | tf_op jit(solution)/shard_map/counts/pallas_call | solution.py:103
  68.8 0.6 fusion.4.pos_ref
  69.4 0.0 all-to-all-done
  69.4 0.0 copy-start.3
  69.4 11.5 %plane_sum.1 = bf16[1024,256]{1,0:T(8,128)(2,1)} custom-call(bf16[8,512,1024]{2,1,0:T(8,128)(2,1)} %counts.1.count_hbm, bf16[8192,256]{1,0:T(8,128)(2,1)} %bitcast.5.bags_hbm, s32[8,512]{1,0:T(8,128)} %fusion.4.pos_ref), custom_call_target="tpu_custom_call" | custom-call | flops 4294967296 | bytes 12582912 | tf_op jit(solution)/shard_map/plane_sum/pallas_call | solution.py:162
  80.9 16.4 %all-to-all-start.1 = ((bf16[8,128,256]{2,1,0:T(8,128)(2,1)}), bf16[8,128,256]{2,1,0:T(8,128)(2,1)S(1)}, u32[]{:S(2)}, u32[]{:S(2)}) async-start(bf16[8,128,256]{2,1,0:T(8,128)(2,1)} %bitcast.32), calls=%async_computation.1 | async-start | bytes 1048576 | tf_op jit(solution)/shard_map/all_to_all | solution.py:208
  97.3 0.0 copy-done.3
  97.3 0.0 copy-done
  97.4 6.2 %gather_fusion.1 = f32[1024]{0:T(1024)S(1)} fusion(f32[4096]{0:T(1024)S(1)} %bitcast.26, s32[1024]{0:T(1024)S(1)} %broadcast_clamp_fusion), kind=kCustom, calls=%fused_computation.1 | custom fusion | bytes 12288 | tf_op jit(solution)/shard_map/jit(_take)/gather | solution.py:210
  103.5 5.7 %gather_fusion = f32[1024,256]{1,0:T(8,128)S(1)} fusion(f32[4096,256]{1,0:T(8,128)} %bitcast.29, s32[1024]{0:T(1024)S(1)} %broadcast_clamp_fusion), kind=kCustom, calls=%fused_computation | custom fusion | bytes 2101248 | tf_op jit(solution)/shard_map/jit(_take)/gather | solution.py:209
  109.2 0.2 broadcast_select_fusion
  109.4 5.4 %all-to-all-done.1 = bf16[8,128,256]{2,1,0:T(8,128)(2,1)S(1)} async-done(((bf16[8,128,256]{2,1,0:T(8,128)(2,1)}), bf16[8,128,256]{2,1,0:T(8,128)(2,1)S(1)}, u32[]{:S(2)}, u32[]{:S(2)}) %all-to-all-start.1) | async-done | bytes 524320 | tf_op jit(solution)/shard_map/all_to_all | solution.py:208
  114.8 0.1 reduce_sum.21
  114.9 3.1 %collective-permute-start.1 = (bf16[128,256]{1,0:T(8,128)(2,1)S(1)}, bf16[128,256]{1,0:T(8,128)(2,1)S(1)}, u32[]{:S(2)}, u32[]{:S(2)}) collective-permute-start(bf16[128,256]{1,0:T(8,128)(2,1)S(1)} %reduce_sum.21), channel_id=1, source_target_pairs={{0,0},{1,8},{2,16},{3,24},{4,32},{5,40},{6,48},{7,56},{8,1},{9,9},... | collective-permute-start | bytes 196616 | tf_op jit(solution)/shard_map/ppermute | solution.py:213
  117.9 2.7 %collective-permute-done.1 = bf16[128,256]{1,0:T(8,128)(2,1)S(1)} collective-permute-done((bf16[128,256]{1,0:T(8,128)(2,1)S(1)}, bf16[128,256]{1,0:T(8,128)(2,1)S(1)}, u32[]{:S(2)}, u32[]{:S(2)}) %collective-permute-start.1) | collective-permute-done | bytes 65568 | tf_op jit(solution)/shard_map/ppermute | solution.py:213
  120.6 17.5 %all_gather.11 = bf16[1024,256]{1,0:T(8,128)(2,1)S(1)} all-gather(bf16[128,256]{1,0:T(8,128)(2,1)S(1)} %collective-permute-done.1), channel_id=1, replica_groups=mesh['y'=4,'z'=8,'x'=4,'core'=2] {'x','core'}, dimensions={0}, use_global_device_ids=true | all-gather | bytes 589824 | tf_op jit(solution)/shard_map/all_gather | solution.py:214
  138.1 0.2 fusion.3
  138.3 0.6 sqrt_add_fusion
  138.9 1.2 fusion.2
  (6 shorter events, 0.1 us)
Async XLA Ops:
  0.6 96.7 %copy-start = (f32[1,4096]{1,0:T(1,128)S(1)}, f32[1,4096]{1,0:T(1,128)}, u32[]{:S(2)}) copy-start(f32[1,4096]{1,0:T(1,128)} %param.13) | copy-start | bytes 49156
  6.3 8.8 %copy-start.1 = (s32[8192,1,8]{0,2,1:T(8,128)S(1)}, s32[8192,1,8]{0,2,1:T(8,128)}, u32[]{:S(2)}) copy-start(s32[8192,1,8]{0,2,1:T(8,128)} %param.9) | copy-start | bytes 786436
  6.3 8.8 %copy-start.2 = (s32[1,1,512]{2,1,0:T(1,128)S(1)}, s32[1,1,512]{2,1,0:T(1,128)}, u32[]{:S(2)}) copy-start(s32[1,1,512]{2,1,0:T(1,128)} %param.10) | copy-start | bytes 6148
  6.3 63.1 %all-to-all-start = ((bf16[32,256,256]{2,1,0:T(8,128)(2,1)}), bf16[32,256,256]{2,1,0:T(8,128)(2,1)}, u32[]{:S(2)}, u32[]{:S(2)}) async-start(bf16[32,256,256]{2,1,0:T(8,128)(2,1)} %mask.1), calls=%async_computation | async-start | bytes 8388608 | tf_op jit(solution)/shard_map/all_to_all | solution.py:202
  15.1 7.0 %collective-permute-start = (s16[9,8,1024]{2,1,0:T(8,128)(2,1)S(1)}, s16[9,8,1024]{2,1,0:T(8,128)(2,1)S(1)}, u32[]{:S(2)}, u32[]{:S(2)}) collective-permute-start(s16[9,8,1024]{2,1,0:T(8,128)(2,1)S(1)} %convert_element_type.18), channel_id=1, source_target_pairs={{0,0},{1,8},{2,16},{3,24},{4,32},{5,40},{6,48},{7,56},{8,1},{9,9},... | collective-permute-start | bytes 442376 | tf_op jit(solution)/shard_map/ppermute | solution.py:195
  69.4 27.9 %copy-start.3 = (s32[1,1024]{1,0:T(1,128)S(1)}, s32[1,1024]{1,0:T(1,128)}, u32[]{:S(2)}) copy-start(s32[1,1024]{1,0:T(1,128)} %param.11) | copy-start | bytes 12292
  80.9 33.8 %all-to-all-start.1 = ((bf16[8,128,256]{2,1,0:T(8,128)(2,1)}), bf16[8,128,256]{2,1,0:T(8,128)(2,1)S(1)}, u32[]{:S(2)}, u32[]{:S(2)}) async-start(bf16[8,128,256]{2,1,0:T(8,128)(2,1)} %bitcast.32), calls=%async_computation.1 | async-start | bytes 1048576 | tf_op jit(solution)/shard_map/all_to_all | solution.py:208
  114.9 5.8 %collective-permute-start.1 = (bf16[128,256]{1,0:T(8,128)(2,1)S(1)}, bf16[128,256]{1,0:T(8,128)(2,1)S(1)}, u32[]{:S(2)}, u32[]{:S(2)}) collective-permute-start(bf16[128,256]{1,0:T(8,128)(2,1)S(1)} %reduce_sum.21), channel_id=1, source_target_pairs={{0,0},{1,8},{2,16},{3,24},{4,32},{5,40},{6,48},{7,56},{8,1},{9,9},... | collective-permute-start | bytes 196616 | tf_op jit(solution)/shard_map/ppermute | solution.py:213

commit v3 on v2

v3 whole, which is shorter than its diff:
```python
import functools

import jax
import jax.numpy as jnp
from jax import lax
from jax.experimental import pallas as pl
from jax.experimental.pallas import tpu as pltpu
from jax.sharding import Mesh
from jax.sharding import PartitionSpec as P

LEARN_RATE = 0.5
ADAGRAD_EPS = 1e-08
REP = ("x", "core")
MIB = 1 << 20


def mask_kernel(n_z, count_ref, grad_ref, out_ref):
    tables, samples, width = out_ref.shape
    n_y = tables // n_z
    first = pl.program_id(0) * samples
    to = lax.broadcasted_iota(jnp.int32, (256, 256), 0)
    source = lax.broadcasted_iota(jnp.int32, (256, 256), 1)
    permute = ((source % 16) * 16 + source // 16 == to).astype(jnp.bfloat16)
    position = lax.broadcasted_iota(jnp.int32, (16, width), 0) + first
    for sample in range(0, samples, 16):
        for table in range(0, tables, 16):
            rows = grad_ref[sample : sample + 16, table : table + 16, :].reshape(256, width)
            moved = jnp.dot(permute, rows.astype(jnp.bfloat16), preferred_element_type=jnp.float32)
            for j in range(16):
                present = position + sample < count_ref[0, table + j]
                kept = jnp.where(present, moved[j * 16 : j * 16 + 16], 0.0)
                place = (table + j) % n_z * n_y + (table + j) // n_z
                out_ref[place, sample : sample + 16, :] = kept.astype(jnp.bfloat16)


def masked_by_table(n_z, pooled_grad, present_count):
    batch, tables, width = pooled_grad.shape
    samples = 128
    return pl.pallas_call(
        functools.partial(mask_kernel, n_z),
        grid=(batch // samples,),
        out_shape=jax.ShapeDtypeStruct((tables, batch, width), jnp.bfloat16),
        in_specs=[
            pl.BlockSpec(memory_space=pltpu.SMEM),
            pl.BlockSpec((samples, tables, width), lambda i: (i, 0, 0)),
        ],
        out_specs=pl.BlockSpec((tables, samples, width), lambda i: (0, i, 0)),
        compiler_params=pltpu.CompilerParams(vmem_limit_bytes=56 * MIB),
        cost_estimate=pl.CostEstimate(flops=batch * tables * width, bytes_accessed=batch * tables * width * 6, transcendentals=0),
        name="mask",
    )(present_count, pooled_grad)


def place_kernel(z_ref, members_ref, pos_ref, out_ref):
    n_z, slots, wide = out_ref.shape
    n_y = wide // 256
    parts = [jnp.broadcast_to(pos_ref[:, pl.ds(128 * k, 128)], (slots, 128)) for k in range(pos_ref.shape[1] // 128)]
    for j in range(n_z):
        z = lax.bitwise_xor(z_ref[0], j)
        for y in range(n_y):
            for half in range(2):
                start = pl.multiple_of((y * n_z + z) * 256 + half * 128, 128)
                member = members_ref[:, pl.ds(start, 128)]
                low, high = member & 127, member >> 7
                found = jnp.take_along_axis(parts[0], low, axis=1)
                for k in range(1, len(parts)):
                    found = jnp.where(high == k, jnp.take_along_axis(parts[k], low, axis=1), found)
                out_ref[j, :, pl.ds(y * 256 + half * 128, 128)] = found


def places_of(members, rep_pos, z, n_z):
    batch, slots = members.shape
    return pl.pallas_call(
        place_kernel,
        out_shape=jax.ShapeDtypeStruct((n_z, slots, batch // n_z), jnp.int32),
        in_specs=[
            pl.BlockSpec(memory_space=pltpu.SMEM),
            pl.BlockSpec(memory_space=pltpu.VMEM),
            pl.BlockSpec(memory_space=pltpu.VMEM),
        ],
        compiler_params=pltpu.CompilerParams(vmem_limit_bytes=8 * MIB),
        cost_estimate=pl.CostEstimate(flops=batch * slots * 8, bytes_accessed=batch * slots * 8, transcendentals=0),
        name="places",
    )(z, members.T, rep_pos)


def turn(v):
    return (v * 2) ^ (v // 4 * 11)


def from_turn(v):
    return (v ^ ((v & 1) * 11)) >> 1


def exchange_over_z(places):
    n_z = places.shape[0]
    places = places.reshape((2, 2, 2) + places.shape[1:])
    for axis, bit in enumerate((4, 2, 1)):
        stay = lax.index_in_dim(places, 0, axis, False)
        go = lax.index_in_dim(places, 1, axis, False)
        come = lax.ppermute(go, "z", [(z, z ^ bit) for z in range(n_z)])
        places = jnp.stack([stay, come], axis)
    return places.reshape((n_z,) + places.shape[3:])


def gather_over_rep(part, n_x):
    x = lax.axis_index("x")
    place = (lax.broadcasted_iota(jnp.int32, (n_x, 1, 1), 0) - x + n_x) % n_x
    rows = part[None]
    for step in range(1, n_x):
        come = lax.ppermute(part, "x", [(a, (a - step) % n_x) for a in range(n_x)])
        rows = jnp.where(place == step, come[None], rows)
    return lax.all_gather(rows, "core", axis=1, tiled=False).reshape(-1, part.shape[1])


def one_hot_rows(values, row):
    return jnp.where(jnp.broadcast_to(values, row.shape) == row, jnp.bfloat16(1), jnp.bfloat16(0))


def count_kernel(place_ref, out_ref):
    slots, samples = place_ref.shape[1:]
    rows = 32
    base = lax.broadcasted_iota(jnp.int32, (rows, 128), 0).astype(jnp.bfloat16)

    def lanes(i, carry):
        at = pl.ds(pl.multiple_of(i * 128, 128), 128)
        place = place_ref[0, :, at]
        high, low = place >> 8, place & 255
        for block in range(out_ref.shape[1] // 256):
            wanted = jnp.where(high == block, low, -1).astype(jnp.bfloat16)
            for first in range(0, 256, rows):
                row = base + jnp.bfloat16(first)
                total = one_hot_rows(wanted[0:1], row)
                for s in range(1, slots):
                    total = total + one_hot_rows(wanted[s : s + 1], row)
                out_ref[0, pl.ds(block * 256 + first, rows), at] = total
        return carry

    lax.fori_loop(0, samples // 128, lanes, 0)


def counts_of(places, active):
    reps, slots, wide = places.shape
    return pl.pallas_call(
        count_kernel,
        grid=(reps,),
        in_specs=[pl.BlockSpec((1, slots, wide), lambda j: (j, 0, 0))],
        out_specs=pl.BlockSpec((1, active, wide), lambda j: (j, 0, 0)),
        out_shape=jax.ShapeDtypeStruct((reps, active, wide), jnp.bfloat16),
        compiler_params=pltpu.CompilerParams(vmem_limit_bytes=56 * MIB),
        cost_estimate=pl.CostEstimate(flops=active * wide * reps * slots * 3, bytes_accessed=active * wide * reps * 2, transcendentals=0),
        name="counts",
    )(places)


AHEAD = 4


def plane_kernel(z_ref, rep_ref, count_hbm, bags_hbm, out_ref, count_buf, bags_buf, total_ref, count_sem, bags_sem):
    reps, _, samples = count_hbm.shape

    def copies(j):
        slot = lax.rem(j, AHEAD)
        group = rep_ref[0] ^ from_turn(z_ref[0] ^ j ^ rep_ref[0])
        start = pl.multiple_of(group * samples, samples)
        return (
            pltpu.make_async_copy(count_hbm.at[j], count_buf.at[slot], count_sem.at[slot]),
            pltpu.make_async_copy(bags_hbm.at[pl.ds(start, samples), :], bags_buf.at[slot], bags_sem.at[slot]),
        )

    for j in range(AHEAD - 1):
        for copy in copies(jnp.int32(j)):
            copy.start()
    total_ref[...] = jnp.zeros_like(total_ref)

    def step(j, carry):
        @pl.when(j + AHEAD - 1 < reps)
        def _():
            for copy in copies(j + AHEAD - 1):
                copy.start()

        for copy in copies(j):
            copy.wait()
        slot = lax.rem(j, AHEAD)
        total_ref[...] += jnp.dot(count_buf[slot], bags_buf[slot], preferred_element_type=jnp.float32)
        return carry

    lax.fori_loop(0, reps, step, 0)
    out_ref[...] = total_ref[...].astype(jnp.bfloat16)


def plane_sum(z, rep, counts, bags):
    reps, active, samples = counts.shape
    width = bags.shape[1]
    return pl.pallas_call(
        plane_kernel,
        out_shape=jax.ShapeDtypeStruct((active, width), jnp.bfloat16),
        in_specs=[
            pl.BlockSpec(memory_space=pltpu.SMEM),
            pl.BlockSpec(memory_space=pltpu.SMEM),
            pl.BlockSpec(memory_space=pl.ANY),
            pl.BlockSpec(memory_space=pl.ANY),
        ],
        out_specs=pl.BlockSpec(memory_space=pltpu.VMEM),
        scratch_shapes=[
            pltpu.VMEM((AHEAD, active, samples), jnp.bfloat16),
            pltpu.VMEM((AHEAD, samples, width), jnp.bfloat16),
            pltpu.VMEM((active, width), jnp.float32),
            pltpu.SemaphoreType.DMA((AHEAD,)),
            pltpu.SemaphoreType.DMA((AHEAD,)),
        ],
        compiler_params=pltpu.CompilerParams(vmem_limit_bytes=56 * MIB),
        cost_estimate=pl.CostEstimate(
            flops=2 * reps * active * samples * width,
            bytes_accessed=reps * samples * (active + width) * 2,
            transcendentals=0,
        ),
        name="plane_sum",
    )(z, rep, counts, bags)


def local(n_z, n_rep, pooled_grad, present_count, members, rep_pos, row_ids, table, accum):
    active, width = row_ids.shape[1], pooled_grad.shape[2]
    swap = [(z * n_rep + q, q * n_z + z) for z in range(n_z) for q in range(n_rep)]

    z, rep = lax.axis_index("z"), lax.axis_index(REP)
    spread = [(a * n_rep + r, (a ^ turn(r ^ a)) * n_rep + a) for a in range(n_z) for r in range(n_rep)]
    plane = z ^ turn(z ^ rep)
    places = places_of(members[:, 0, :], rep_pos[0], plane.reshape(1), n_z).astype(jnp.int16)
    places = lax.ppermute(places, ("z",) + REP, spread)
    places = exchange_over_z(places).astype(jnp.int32)

    masked = masked_by_table(n_z, pooled_grad, present_count)
    arrived = lax.all_to_all(masked, REP + ("y",), split_axis=0, concat_axis=0, tiled=True)

    counts = counts_of(places, active)
    partial = plane_sum(z.reshape(1), rep.reshape(1), counts, arrived.reshape(-1, width))

    chunks = partial.reshape(n_z, active // n_z, width)
    chunks = lax.all_to_all(chunks, "z", split_axis=0, concat_axis=0, tiled=True)
    old_rows = jnp.take(table[0], row_ids[0], axis=0)
    old_state = jnp.take(accum[0], row_ids[0], axis=0)
    chunks, old_rows, old_state = lax.optimization_barrier((chunks, old_rows, old_state))
    part = jnp.sum(chunks.astype(jnp.float32), axis=0).astype(jnp.bfloat16)
    part = lax.ppermute(part, ("z",) + REP, swap)
    summed = gather_over_rep(part, n_rep // 2).astype(jnp.float32)

    new_state = old_state + jnp.mean(summed * summed, axis=1)
    updated = old_rows - LEARN_RATE * summed / (jnp.sqrt(new_state)[:, None] + ADAGRAD_EPS)
    return (updated[None], new_state[None])


def solution(mesh):
    n_y, n_z, n_x, n_core = 4, 8, 4, 2
    grid = Mesh(mesh.devices.reshape(n_y, n_z, n_x, n_core), ("y", "z", "x", "core"))
    shard = ("y", "z")
    in_specs = (
        P(REP + shard, None, None),
        P(REP + shard, None),
        P(REP, shard, None),
        P(REP, shard, None),
        P(shard, None),
        P(shard, None, None),
        P(shard, None),
    )
    out_specs = (P(shard, None, None), P(shard, None))
    return jax.shard_map(
        functools.partial(local, n_z, n_x * n_core),
        mesh=grid,
        in_specs=in_specs,
        out_specs=out_specs,
        check_vma=False,
    )
```

time: 141 us -> 129 us (0.915)
  blocking collectives: 53.7 us -> 6.24 us
  waiting for transfers between devices: 11.3 us -> 28.9 us
  starting transfers between devices: 32 us -> 45.6 us
  Pallas kernels: 26.9 us -> 32.1 us
    all_gather x2 -> x1, blocking collectives: 53.7 us -> 6.24 us  [gather_over_rep(): lax.all_gather(rows, 'core', axis=1, tiled=False).reshape(-1, part.shape[1])]
    ppermute x1 -> x7, starting transfers between devices: 3.74 us -> 24.8 us  [the longest x3 10.4 us: exchange_over_z(): come = lax.ppermute(go, 'z', [(z, z ^ bit) for z in range(n_z)])]
    ppermute x1 -> x7, waiting for transfers between devices: 3.21 us -> 19.5 us  [the longest x3 10.7 us: exchange_over_z(): come = lax.ppermute(go, 'z', [(z, z ^ bit) for z in range(n_z)])]
    all_to_all x1, starting transfers between devices: 16.4 us -> 8.01 us  [local(): lax.all_to_all(chunks, 'z', split_axis=0, concat_axis=0, tiled=True)]
    pallas_call x1, Pallas kernels: 9.7 us -> 17.1 us  [counts_of(): pl.pallas_call(count_kernel, grid=(reps,), in_specs=[pl.BlockSpec((1, slo...]
    all_to_all x1, waiting for transfers between devices: 0.01 us -> 3.08 us  [local(): lax.all_to_all(masked, REP + ('y',), split_axis=0, concat_axis=0, tiled=T...]
    pallas_call x1, Pallas kernels: 11.5 us -> 8.98 us  [plane_sum(): pl.pallas_call(plane_kernel, out_shape=jax.ShapeDtypeStruct((active, widt...]
  transfers between devices with their start and end apart: 4 -> 10, of which waited for: 3 -> 10; matrix products, arithmetic and copies ran while one was open for 10% -> 10% of each run, Pallas kernels for 7% -> 14%
where the time goes in v3:
time: 129 us
  starting transfers between devices  45.6 us (35%)
  Pallas kernels  32.1 us (25%)
  waiting for transfers between devices  28.9 us (22%)
  local copies, waits for them, and re-layouts  11.8 us (9%)
  blocking collectives  6.24 us (5%)
  other arithmetic  3.28 us (3%)
    pallas_call x1, Pallas kernels, counts_of(): pl.pallas_call(count_kernel, grid=(reps,), in_specs=[pl.BlockSpec((1, slo...  17.1 us
    ppermute x3, waiting for transfers between devices, exchange_over_z(): come = lax.ppermute(go, 'z', [(z, z ^ bit) for z in range(n_z)])  10.7 us
    ppermute x3, starting transfers between devices, exchange_over_z(): come = lax.ppermute(go, 'z', [(z, z ^ bit) for z in range(n_z)])  10.4 us
    ppermute x3, starting transfers between devices, gather_over_rep(): come = lax.ppermute(part, 'x', [(a, (a - step) % n_x) for a in range(n_x)])  9.31 us
    pallas_call x1, Pallas kernels, plane_sum(): pl.pallas_call(plane_kernel, out_shape=jax.ShapeDtypeStruct((active, widt...  8.98 us
    all_to_all x1, starting transfers between devices, local(): lax.all_to_all(masked, REP + ('y',), split_axis=0, concat_axis=0, tiled=T...  8.78 us
    all_to_all x1, starting transfers between devices, local(): lax.all_to_all(chunks, 'z', split_axis=0, concat_axis=0, tiled=True)  8.01 us
    all_gather x1, blocking collectives, gather_over_rep(): lax.all_gather(rows, 'core', axis=1, tiled=False).reshape(-1, part.shape[1])  6.24 us
  transfers between devices with their start and end apart: 10, of which 10 were waited for; matrix products, arithmetic and copies ran while one was open for 10% of the time, Pallas kernels for 14%

profile of v3, /device:TPU:1, one launch (start us, length us, event | category | flops | bytes accessed | tf_op | source)
XLA Modules:
  0.0 128.8 jit_solution(4027835056672357784)
XLA Ops:
  0.6 5.5 %mask.1 = bf16[32,256,256]{2,1,0:T(8,128)(2,1)} custom-call(s32[1,32]{1,0:T(1,128)} %count_ref.1, f32[256,32,256]{2,1,0:T(8,128)} %grad_ref.1), custom_call_target="tpu_custom_call" | custom-call | flops 2097152 | bytes 12582912 | tf_op jit(solution)/shard_map/mask/pallas_call | solution.py:39
  6.2 8.8 %all-to-all-start = ((bf16[32,256,256]{2,1,0:T(8,128)(2,1)}), bf16[32,256,256]{2,1,0:T(8,128)(2,1)}, u32[]{:S(2)}, u32[]{:S(2)}) async-start(bf16[32,256,256]{2,1,0:T(8,128)(2,1)} %mask.1), calls=%async_computation | async-start | bytes 8388608 | tf_op jit(solution)/shard_map/all_to_all | solution.py:234
  15.0 0.5 places.1
  15.6 5.1 %collective-permute-start = (s16[8,8,1024]{2,1,0:T(8,128)(2,1)S(1)}, s16[8,8,1024]{2,1,0:T(8,128)(2,1)S(1)}, u32[]{:S(2)}, u32[]{:S(2)}) collective-permute-start(s16[8,8,1024]{2,1,0:T(8,128)(2,1)S(1)} %convert_element_type.15), channel_id=1, source_target_pairs={{0,0},{1,16},{2,32},{3,48},{4,24},{5,8},{6,56},{7,40},{8,25},{9,9}... | collective-permute-start | bytes 393224 | tf_op jit(solution)/shard_map/ppermute | solution.py:230
  20.7 4.4 %collective-permute-done = s16[8,8,1024]{2,1,0:T(8,128)(2,1)S(1)} collective-permute-done((s16[8,8,1024]{2,1,0:T(8,128)(2,1)S(1)}, s16[8,8,1024]{2,1,0:T(8,128)(2,1)S(1)}, u32[]{:S(2)}, u32[]{:S(2)}) %collective-permute-start) | collective-permute-done | bytes 131104 | tf_op jit(solution)/shard_map/ppermute | solution.py:230
  25.1 9.6 %collective-permute-start.1 = (s16[2,2,8,1024]{3,2,1,0:T(8,128)(2,1)S(1)}, s16[2,2,8,1024]{3,2,1,0:T(8,128)(2,1)S(1)}, u32[]{:S(2)}, u32[]{:S(2)}) collective-permute-start(s16[2,2,8,1024]{3,2,1,0:T(8,128)(2,1)S(1)} %bitcast.49), channel_id=1, source_target_pairs={{0,32},{8,40},{16,48},{24,56},{32,0},{40,8},{48,16},{56,24},{1,33}... | collective-permute-start | bytes 196616 | tf_op jit(solution)/shard_map/ppermute | solution.py:101
  34.7 2.4 %collective-permute-done.1 = s16[2,2,8,1024]{3,2,1,0:T(8,128)(2,1)S(1)} collective-permute-done((s16[2,2,8,1024]{3,2,1,0:T(8,128)(2,1)S(1)}, s16[2,2,8,1024]{3,2,1,0:T(8,128)(2,1)S(1)}, u32[]{:S(2)}, u32[]{:S(2)}) %collective-permute-start.1) | collective-permute-done | bytes 65568 | tf_op jit(solution)/shard_map/ppermute | solution.py:101
  37.2 0.7 collective-permute-start.2
  37.8 4.7 %collective-permute-done.2 = s16[2,2,8,1024]{3,2,0,1:T(8,128)(2,1)S(1)} collective-permute-done((s16[2,2,8,1024]{3,2,0,1:T(8,128)(2,1)S(1)}, s16[2,2,8,1024]{3,2,0,1:T(8,128)(2,1)S(1)}, u32[]{:S(2)}, u32[]{:S(2)}) %collective-permute-start.2) | collective-permute-done | bytes 65568 | tf_op jit(solution)/shard_map/ppermute | solution.py:101
  42.6 0.1 collective-permute-start.3
  42.7 3.5 %collective-permute-done.3 = s16[2,2,8,1024]{3,2,1,0:T(8,128)(2,1)S(1)} collective-permute-done((s16[2,2,8,1024]{3,2,1,0:T(8,128)(2,1)S(1)}, s16[2,2,8,1024]{3,2,1,0:T(8,128)(2,1)S(1)}, u32[]{:S(2)}, u32[]{:S(2)}) %collective-permute-start.3) | collective-permute-done | bytes 65568 | tf_op jit(solution)/shard_map/ppermute | solution.py:101
  46.2 0.7 bitcast_convert_fusion.place_ref
  46.9 17.1 %counts.1.count_hbm = bf16[8,1024,1024]{2,1,0:T(8,128)(2,1)} custom-call(s32[8,8,1024]{2,1,0:T(8,128)} %bitcast_convert_fusion.place_ref), custom_call_target="tpu_custom_call" | custom-call | flops 201326592 | bytes 16777216 | tf_op jit(solution)/shard_map/counts/pallas_call | solution.py:144
  64.0 3.1 %all-to-all-done = bf16[32,256,256]{2,1,0:T(8,128)(2,1)} async-done(((bf16[32,256,256]{2,1,0:T(8,128)(2,1)}), bf16[32,256,256]{2,1,0:T(8,128)(2,1)}, u32[]{:S(2)}, u32[]{:S(2)}) %all-to-all-start) | async-done | bytes 4194336 | tf_op jit(solution)/shard_map/all_to_all | solution.py:234
  67.1 9.0 %plane_sum.1 = bf16[1024,256]{1,0:T(8,128)(2,1)} custom-call(s32[1]{0:T(128)} %bitcast.z_ref, s32[1]{0:T(128)} %bitcast.1.rep_ref, bf16[8,1024,1024]{2,1,0:T(8,128)(2,1)} %counts.1.count_hbm, bf16[8192,256]{1,0:T(8,128)(2,1)} %bitcast.17.bags_hbm), custom_call_target="tpu_custom_call" | custom-call | flops 4294967296 | bytes 20971520 | tf_op jit(solution)/shard_map/plane_sum/pallas_call | solution.py:195
  76.1 8.0 %all-to-all-start.1 = ((bf16[8,128,256]{2,1,0:T(8,128)(2,1)}), bf16[8,128,256]{2,1,0:T(8,128)(2,1)S(1)}, u32[]{:S(2)}, u32[]{:S(2)}) async-start(bf16[8,128,256]{2,1,0:T(8,128)(2,1)} %bitcast.44), calls=%async_computation.1 | async-start | bytes 1048576 | tf_op jit(solution)/shard_map/all_to_all | solution.py:240
  84.1 6.2 %gather_fusion.1 = f32[1024]{0:T(1024)S(1)} fusion(f32[4096]{0:T(1024)S(1)} %bitcast.40, s32[1024]{0:T(1024)S(1)} %broadcast_clamp_fusion), kind=kCustom, calls=%fused_computation.1 | custom fusion | bytes 12288 | tf_op jit(solution)/shard_map/jit(_take)/gather | solution.py:242
  90.3 5.7 %gather_fusion = f32[1024,256]{1,0:T(8,128)S(1)} fusion(f32[4096,256]{1,0:T(8,128)} %bitcast.43, s32[1024]{0:T(1024)S(1)} %broadcast_clamp_fusion), kind=kCustom, calls=%fused_computation | custom fusion | bytes 2101248 | tf_op jit(solution)/shard_map/jit(_take)/gather | solution.py:241
  95.9 0.2 broadcast_select_fusion
  96.2 4.4 %all-to-all-done.1 = bf16[8,128,256]{2,1,0:T(8,128)(2,1)S(1)} async-done(((bf16[8,128,256]{2,1,0:T(8,128)(2,1)}), bf16[8,128,256]{2,1,0:T(8,128)(2,1)S(1)}, u32[]{:S(2)}, u32[]{:S(2)}) %all-to-all-start.1) | async-done | bytes 524320 | tf_op jit(solution)/shard_map/all_to_all | solution.py:240
  100.7 4.0 %collective-permute-start.4 = (bf16[128,256]{1,0:T(8,128)(2,1)S(1)}, bf16[128,256]{1,0:T(8,128)(2,1)S(1)}, u32[]{:S(2)}, u32[]{:S(2)}) collective-permute-start(bf16[128,256]{1,0:T(8,128)(2,1)S(1)} %reduce_sum.21), channel_id=1, source_target_pairs={{0,0},{1,8},{2,16},{3,24},{4,32},{5,40},{6,48},{7,56},{8,1},{9,9},... | collective-permute-start | bytes 196616 | tf_op jit(solution)/shard_map/ppermute | solution.py:245
  104.7 1.9 %collective-permute-done.4 = bf16[128,256]{1,0:T(8,128)(2,1)S(1)} collective-permute-done((bf16[128,256]{1,0:T(8,128)(2,1)S(1)}, bf16[128,256]{1,0:T(8,128)(2,1)S(1)}, u32[]{:S(2)}, u32[]{:S(2)}) %collective-permute-start.4) | collective-permute-done | bytes 65568 | tf_op jit(solution)/shard_map/ppermute | solution.py:245
  106.6 8.7 %collective-permute-start.7 = (bf16[128,256]{1,0:T(8,128)(2,1)S(1)}, bf16[128,256]{1,0:T(8,128)(2,1)S(1)}, u32[]{:S(2)}, u32[]{:S(2)}) collective-permute-start(bf16[128,256]{1,0:T(8,128)(2,1)S(1)} %collective-permute-done.4), channel_id=1, source_target_pairs={{0,6},{2,0},{4,2},{6,4},{1,7},{3,1},{5,3},{7,5},{8,14},{10,8},{12,... | collective-permute-start | bytes 196616 | tf_op jit(solution)/shard_map/ppermute | solution.py:111
  115.3 0.6 collective-permute-start.5
  115.9 1.3 %collective-permute-done.7 = bf16[128,256]{1,0:T(8,128)(2,1)S(1)} collective-permute-done((bf16[128,256]{1,0:T(8,128)(2,1)S(1)}, bf16[128,256]{1,0:T(8,128)(2,1)S(1)}, u32[]{:S(2)}, u32[]{:S(2)}) %collective-permute-start.7) | collective-permute-done | bytes 65568 | tf_op jit(solution)/shard_map/ppermute | solution.py:111
  117.3 2.8 %collective-permute-done.6 = bf16[128,256]{1,0:T(8,128)(2,1)S(1)} collective-permute-done((bf16[128,256]{1,0:T(8,128)(2,1)S(1)}, bf16[128,256]{1,0:T(8,128)(2,1)S(1)}, u32[]{:S(2)}, u32[]{:S(2)}) %collective-permute-start.6) | collective-permute-done | bytes 65568 | tf_op jit(solution)/shard_map/ppermute | solution.py:111
  120.1 0.3 collective-permute-done.5
  120.4 0.1 select_select_fusion
  120.5 6.2 %all_gather.4 = bf16[4,2,128,256]{3,2,1,0:T(8,128)(2,1)S(1)} all-gather(bf16[4,1,128,256]{3,2,1,0:T(8,128)(2,1)S(1)} %select_select_fusion), channel_id=1, replica_groups=mesh['y'=4,'z'=8,'x'=4,'core'=2] {'core'}, dimensions={1}, use_global_device_ids=true | all-gather | bytes 786432 | tf_op jit(solution)/shard_map/all_gather | solution.py:113
  126.7 0.2 fusion
  127.0 0.6 sqrt_add_fusion
  127.6 1.2 fusion.1
  (21 shorter events, 0.2 us)
Async XLA Ops:
  0.6 83.5 %copy-start = (f32[1,4096]{1,0:T(1,128)S(1)}, f32[1,4096]{1,0:T(1,128)}, u32[]{:S(2)}) copy-start(f32[1,4096]{1,0:T(1,128)} %param.13) | copy-start | bytes 49156
  6.2 8.8 %copy-start.1 = (s32[8192,1,8]{0,2,1:T(8,128)S(1)}, s32[8192,1,8]{0,2,1:T(8,128)}, u32[]{:S(2)}) copy-start(s32[8192,1,8]{0,2,1:T(8,128)} %param.9) | copy-start | bytes 786436
  6.2 8.8 %copy-start.2 = (s32[1,1,512]{2,1,0:T(1,128)S(1)}, s32[1,1,512]{2,1,0:T(1,128)}, u32[]{:S(2)}) copy-start(s32[1,1,512]{2,1,0:T(1,128)} %param.10) | copy-start | bytes 6148
  6.2 60.9 %all-to-all-start = ((bf16[32,256,256]{2,1,0:T(8,128)(2,1)}), bf16[32,256,256]{2,1,0:T(8,128)(2,1)}, u32[]{:S(2)}, u32[]{:S(2)}) async-start(bf16[32,256,256]{2,1,0:T(8,128)(2,1)} %mask.1), calls=%async_computation | async-start | bytes 8388608 | tf_op jit(solution)/shard_map/all_to_all | solution.py:234
  15.6 9.5 %collective-permute-start = (s16[8,8,1024]{2,1,0:T(8,128)(2,1)S(1)}, s16[8,8,1024]{2,1,0:T(8,128)(2,1)S(1)}, u32[]{:S(2)}, u32[]{:S(2)}) collective-permute-start(s16[8,8,1024]{2,1,0:T(8,128)(2,1)S(1)} %convert_element_type.15), channel_id=1, source_target_pairs={{0,0},{1,16},{2,32},{3,48},{4,24},{5,8},{6,56},{7,40},{8,25},{9,9}... | collective-permute-start | bytes 393224 | tf_op jit(solution)/shard_map/ppermute | solution.py:230
  25.1 12.1 %collective-permute-start.1 = (s16[2,2,8,1024]{3,2,1,0:T(8,128)(2,1)S(1)}, s16[2,2,8,1024]{3,2,1,0:T(8,128)(2,1)S(1)}, u32[]{:S(2)}, u32[]{:S(2)}) collective-permute-start(s16[2,2,8,1024]{3,2,1,0:T(8,128)(2,1)S(1)} %bitcast.49), channel_id=1, source_target_pairs={{0,32},{8,40},{16,48},{24,56},{32,0},{40,8},{48,16},{56,24},{1,33}... | collective-permute-start | bytes 196616 | tf_op jit(solution)/shard_map/ppermute | solution.py:101
  37.2 5.4 %collective-permute-start.2 = (s16[2,2,8,1024]{3,2,0,1:T(8,128)(2,1)S(1)}, s16[2,2,8,1024]{3,2,0,1:T(8,128)(2,1)S(1)}, u32[]{:S(2)}, u32[]{:S(2)}) collective-permute-start(s16[2,2,8,1024]{3,2,0,1:T(8,128)(2,1)S(1)} %get-tuple-element.17), channel_id=1, source_target_pairs={{0,16},{8,24},{16,0},{24,8},{32,48},{40,56},{48,32},{56,40},{1,17}... | collective-permute-start | bytes 196616 | tf_op jit(solution)/shard_map/ppermute | solution.py:101
  42.6 3.6 %collective-permute-start.3 = (s16[2,2,8,1024]{3,2,1,0:T(8,128)(2,1)S(1)}, s16[2,2,8,1024]{3,2,1,0:T(8,128)(2,1)S(1)}, u32[]{:S(2)}, u32[]{:S(2)}) collective-permute-start(s16[2,2,8,1024]{3,2,1,0:T(8,128)(2,1)S(1)} %get-tuple-element.15), channel_id=1, source_target_pairs={{0,8},{8,0},{16,24},{24,16},{32,40},{40,32},{48,56},{56,48},{1,9},... | collective-permute-start | bytes 196616 | tf_op jit(solution)/shard_map/ppermute | solution.py:101
  67.1 17.0 %copy-start.3 = (s32[1,1024]{1,0:T(1,128)S(1)}, s32[1,1024]{1,0:T(1,128)}, u32[]{:S(2)}) copy-start(s32[1,1024]{1,0:T(1,128)} %param.11) | copy-start | bytes 12292
  76.1 24.5 %all-to-all-start.1 = ((bf16[8,128,256]{2,1,0:T(8,128)(2,1)}), bf16[8,128,256]{2,1,0:T(8,128)(2,1)S(1)}, u32[]{:S(2)}, u32[]{:S(2)}) async-start(bf16[8,128,256]{2,1,0:T(8,128)(2,1)} %bitcast.44), calls=%async_computation.1 | async-start | bytes 1048576 | tf_op jit(solution)/shard_map/all_to_all | solution.py:240
  100.7 5.9 %collective-permute-start.4 = (bf16[128,256]{1,0:T(8,128)(2,1)S(1)}, bf16[128,256]{1,0:T(8,128)(2,1)S(1)}, u32[]{:S(2)}, u32[]{:S(2)}) collective-permute-start(bf16[128,256]{1,0:T(8,128)(2,1)S(1)} %reduce_sum.21), channel_id=1, source_target_pairs={{0,0},{1,8},{2,16},{3,24},{4,32},{5,40},{6,48},{7,56},{8,1},{9,9},... | collective-permute-start | bytes 196616 | tf_op jit(solution)/shard_map/ppermute | solution.py:245
  106.6 10.6 %collective-permute-start.7 = (bf16[128,256]{1,0:T(8,128)(2,1)S(1)}, bf16[128,256]{1,0:T(8,128)(2,1)S(1)}, u32[]{:S(2)}, u32[]{:S(2)}) collective-permute-start(bf16[128,256]{1,0:T(8,128)(2,1)S(1)} %collective-permute-done.4), channel_id=1, source_target_pairs={{0,6},{2,0},{4,2},{6,4},{1,7},{3,1},{5,3},{7,5},{8,14},{10,8},{12,... | collective-permute-start | bytes 196616 | tf_op jit(solution)/shard_map/ppermute | solution.py:111
  115.3 4.7 %collective-permute-start.6 = (bf16[128,256]{1,0:T(8,128)(2,1)S(1)}, bf16[128,256]{1,0:T(8,128)(2,1)S(1)}, u32[]{:S(2)}, u32[]{:S(2)}) collective-permute-start(bf16[128,256]{1,0:T(8,128)(2,1)S(1)} %collective-permute-done.4), channel_id=1, source_target_pairs={{0,4},{2,6},{4,0},{6,2},{1,5},{3,7},{5,1},{7,3},{8,12},{10,14},{12... | collective-permute-start | bytes 196616 | tf_op jit(solution)/shard_map/ppermute | solution.py:111
  115.3 5.0 %collective-permute-start.5 = (bf16[128,256]{1,0:T(8,128)(2,1)S(1)}, bf16[128,256]{1,0:T(8,128)(2,1)S(1)}, u32[]{:S(2)}, u32[]{:S(2)}) collective-permute-start(bf16[128,256]{1,0:T(8,128)(2,1)S(1)} %collective-permute-done.4), channel_id=1, source_target_pairs={{0,2},{2,4},{4,6},{6,0},{1,3},{3,5},{5,7},{7,1},{8,10},{10,12},{12... | collective-permute-start | bytes 196616 | tf_op jit(solution)/shard_map/ppermute | solution.py:111

commit v4 on v3

--- a/solution.py
+++ b/solution.py
@@ -84,12 +84,32 @@
     )(z, members.T, rep_pos)
 
 
+def state_kernel(ids_ref, accum_ref, out_ref):
+    low, high = ids_ref[...] & 127, ids_ref[...] >> 7
+    found = jnp.zeros(out_ref.shape, jnp.float32)
+    for k in range(accum_ref.shape[0]):
+        row = jnp.broadcast_to(accum_ref[k : k + 1, :], out_ref.shape)
+        found = jnp.where(high == k, jnp.take_along_axis(row, low, axis=1), found)
+    out_ref[...] = found
+
+
+def state_of(accum, row_ids):
+    ids = row_ids.reshape(-1, 128)
+    return pl.pallas_call(
+        state_kernel,
+        out_shape=jax.ShapeDtypeStruct(ids.shape, jnp.float32),
+        compiler_params=pltpu.CompilerParams(vmem_limit_bytes=4 * MIB),
+        cost_estimate=pl.CostEstimate(flops=accum.size * 8, bytes_accessed=accum.size * 4, transcendentals=0),
+        name="state",
+    )(ids, accum.reshape(-1, 128)).reshape(-1)
+
+
 def turn(v):
+    return (v ^ ((v & 1) * 11)) >> 1
+
+
+def from_turn(v):
     return (v * 2) ^ (v // 4 * 11)
-
-
-def from_turn(v):
-    return (v ^ ((v & 1) * 11)) >> 1
 
 
 def exchange_over_z(places):
@@ -101,6 +121,20 @@
         come = lax.ppermute(go, "z", [(z, z ^ bit) for z in range(n_z)])
         places = jnp.stack([stay, come], axis)
     return places.reshape((n_z,) + places.shape[3:])
+
+
+def sum_over_z(even, up, down, across, n_z):
+    def shift(array, by):
+        return lax.ppermute(array, "z", [(a, (a + by) % n_z) for a in range(n_z)])
+
+    def plus(a, b):
+        return a.astype(jnp.float32) + b.astype(jnp.float32)
+
+    up, down, across = shift(up, 1), shift(down, -1), shift(across, 4)
+    two_up = shift(plus(even[1], up[1]).astype(jnp.bfloat16), 2)
+    two_down = shift(plus(even[2], down[0]).astype(jnp.bfloat16), -2)
+    total = plus(even[0], up[0]) + plus(across, down[1]) + plus(two_up, two_down)
+    return total.astype(jnp.bfloat16)
 
 
 def gather_over_rep(part, n_x):
@@ -133,7 +167,7 @@
                 total = one_hot_rows(wanted[0:1], row)
                 for s in range(1, slots):
                     total = total + one_hot_rows(wanted[s : s + 1], row)
-                out_ref[0, pl.ds(block * 256 + first, rows), at] = total
+                out_ref[0, pl.ds(block * 256 + first, rows), at] = total.astype(out_ref.dtype)
         return carry
 
     lax.fori_loop(0, samples // 128, lanes, 0)
@@ -146,9 +180,9 @@
         grid=(reps,),
         in_specs=[pl.BlockSpec((1, slots, wide), lambda j: (j, 0, 0))],
         out_specs=pl.BlockSpec((1, active, wide), lambda j: (j, 0, 0)),
-        out_shape=jax.ShapeDtypeStruct((reps, active, wide), jnp.bfloat16),
+        out_shape=jax.ShapeDtypeStruct((reps, active, wide), jnp.float8_e4m3fn),
         compiler_params=pltpu.CompilerParams(vmem_limit_bytes=56 * MIB),
-        cost_estimate=pl.CostEstimate(flops=active * wide * reps * slots * 3, bytes_accessed=active * wide * reps * 2, transcendentals=0),
+        cost_estimate=pl.CostEstimate(flops=active * wide * reps * slots * 3, bytes_accessed=active * wide * reps, transcendentals=0),
         name="counts",
     )(places)
 
@@ -156,8 +190,9 @@
 AHEAD = 4
 
 
-def plane_kernel(z_ref, rep_ref, count_hbm, bags_hbm, out_ref, count_buf, bags_buf, total_ref, count_sem, bags_sem):
+def plane_kernel(z_ref, rep_ref, count_hbm, bags_hbm, even_ref, up_ref, down_ref, across_ref, count_buf, bags_buf, total_ref, count_sem, bags_sem):
     reps, _, samples = count_hbm.shape
+    n_z, rows = 8, across_ref.shape[0]
 
     def copies(j):
         slot = lax.rem(j, AHEAD)
@@ -182,28 +217,36 @@
         for copy in copies(j):
             copy.wait()
         slot = lax.rem(j, AHEAD)
-        total_ref[...] += jnp.dot(count_buf[slot], bags_buf[slot], preferred_element_type=jnp.float32)
+        counts = count_buf[slot].astype(jnp.bfloat16)
+        total_ref[...] += jnp.dot(counts, bags_buf[slot], preferred_element_type=jnp.float32)
         return carry
 
     lax.fori_loop(0, reps, step, 0)
-    out_ref[...] = total_ref[...].astype(jnp.bfloat16)
-
-
-def plane_sum(z, rep, counts, bags):
+    def rows_for(k):
+        first = pl.multiple_of(lax.rem(z_ref[0] + k, n_z) * rows, rows)
+        return total_ref[pl.ds(first, rows), :].astype(jnp.bfloat16)
+
+    for out_ref, ks in ((even_ref, (0, 2, 6)), (up_ref, (1, 3)), (down_ref, (5, 7))):
+        for place, k in enumerate(ks):
+            out_ref[place] = rows_for(k)
+    across_ref[...] = rows_for(4)
+
+
+def plane_sum(z, rep, counts, bags, n_z):
     reps, active, samples = counts.shape
     width = bags.shape[1]
     return pl.pallas_call(
         plane_kernel,
-        out_shape=jax.ShapeDtypeStruct((active, width), jnp.bfloat16),
+        out_shape=[jax.ShapeDtypeStruct(lead + (active // n_z, width), jnp.bfloat16) for lead in ((3,), (2,), (2,), ())],
         in_specs=[
             pl.BlockSpec(memory_space=pltpu.SMEM),
             pl.BlockSpec(memory_space=pltpu.SMEM),
             pl.BlockSpec(memory_space=pl.ANY),
             pl.BlockSpec(memory_space=pl.ANY),
         ],
-        out_specs=pl.BlockSpec(memory_space=pltpu.VMEM),
+        out_specs=[pl.BlockSpec(memory_space=pltpu.VMEM)] * 4,
         scratch_shapes=[
-            pltpu.VMEM((AHEAD, active, samples), jnp.bfloat16),
+            pltpu.VMEM((AHEAD, active, samples), counts.dtype),
             pltpu.VMEM((AHEAD, samples, width), jnp.bfloat16),
             pltpu.VMEM((active, width), jnp.float32),
             pltpu.SemaphoreType.DMA((AHEAD,)),
@@ -212,7 +255,7 @@
         compiler_params=pltpu.CompilerParams(vmem_limit_bytes=56 * MIB),
         cost_estimate=pl.CostEstimate(
             flops=2 * reps * active * samples * width,
-            bytes_accessed=reps * samples * (active + width) * 2,
+            bytes_accessed=reps * samples * (active + 2 * width),
             transcendentals=0,
         ),
         name="plane_sum",
@@ -228,20 +271,19 @@
     plane = z ^ turn(z ^ rep)
     places = places_of(members[:, 0, :], rep_pos[0], plane.reshape(1), n_z).astype(jnp.int16)
     places = lax.ppermute(places, ("z",) + REP, spread)
-    places = exchange_over_z(places).astype(jnp.int32)
+    places = exchange_over_z(places)
+    old_rows = jnp.take(table[0], row_ids[0], axis=0)
+    old_state = state_of(accum[0], row_ids[0])
+    places, old_rows, old_state = lax.optimization_barrier((places, old_rows, old_state))
+    places = places.astype(jnp.int32)
 
     masked = masked_by_table(n_z, pooled_grad, present_count)
     arrived = lax.all_to_all(masked, REP + ("y",), split_axis=0, concat_axis=0, tiled=True)
 
     counts = counts_of(places, active)
-    partial = plane_sum(z.reshape(1), rep.reshape(1), counts, arrived.reshape(-1, width))
-
-    chunks = partial.reshape(n_z, active // n_z, width)
-    chunks = lax.all_to_all(chunks, "z", split_axis=0, concat_axis=0, tiled=True)
-    old_rows = jnp.take(table[0], row_ids[0], axis=0)
-    old_state = jnp.take(accum[0], row_ids[0], axis=0)
-    chunks, old_rows, old_state = lax.optimization_barrier((chunks, old_rows, old_state))
-    part = jnp.sum(chunks.astype(jnp.float32), axis=0).astype(jnp.bfloat16)
+    partial = plane_sum(z.reshape(1), rep.reshape(1), counts, arrived.reshape(-1, width), n_z)
+
+    part = sum_over_z(*partial, n_z)
     part = lax.ppermute(part, ("z",) + REP, swap)
     summed = gather_over_rep(part, n_rep // 2).astype(jnp.float32)
 

time: 129 us -> 123 us (0.953)
  the two profiles are of different devices: /device:TPU:1 before, /device:TPU:89 now
where the time goes in v4:
time: 123 us
  starting transfers between devices  46.9 us (38%)
  Pallas kernels  30.5 us (25%)
  waiting for transfers between devices  24.3 us (20%)
  blocking collectives  9.81 us (8%)
  local copies, waits for them, and re-layouts  5.68 us (5%)
  other arithmetic  4.96 us (4%)
    pallas_call x1, Pallas kernels, counts_of(): pl.pallas_call(count_kernel, grid=(reps,), in_specs=[pl.BlockSpec((1, slo...  15.9 us
    all_gather x1, blocking collectives, gather_over_rep(): lax.all_gather(rows, 'core', axis=1, tiled=False).reshape(-1, part.shape[1])  9.81 us
    ppermute x3, starting transfers between devices, exchange_over_z(): come = lax.ppermute(go, 'z', [(z, z ^ bit) for z in range(n_z)])  9.77 us
    ppermute x1, starting transfers between devices, local(): part = lax.ppermute(part, ('z',) + REP, swap)  8.84 us
    pallas_call x1, Pallas kernels, plane_sum(): pl.pallas_call(plane_kernel, out_shape=[jax.ShapeDtypeStruct(lead + (acti...  8.36 us
    ppermute x1, starting transfers between devices, local(): places = lax.ppermute(places, ('z',) + REP, spread)  8.17 us
    ppermute x5, starting transfers between devices, shift(): return lax.ppermute(array, 'z', [(a, (a + by) % n_z) for a in range(n_z)])  7.93 us
    all_to_all x1, starting transfers between devices, local(): lax.all_to_all(masked, REP + ('y',), split_axis=0, concat_axis=0, tiled=T...  7.82 us
  transfers between devices with their start and end apart: 14, of which 11 were waited for; matrix products, arithmetic and copies ran while one was open for 6% of the time, Pallas kernels for 13%

profile of v4, /device:TPU:89, one launch (start us, length us, event | category | flops | bytes accessed | tf_op | source)
XLA Modules:
  0.0 123.0 jit_solution(18368926182867870517)
XLA Ops:
  0.6 5.6 %mask.1 = bf16[32,256,256]{2,1,0:T(8,128)(2,1)} custom-call(s32[1,32]{1,0:T(1,128)} %count_ref.1, f32[256,32,256]{2,1,0:T(8,128)} %grad_ref.1), custom_call_target="tpu_custom_call" | custom-call | flops 2097152 | bytes 12582912 | tf_op jit(solution)/shard_map/mask/pallas_call | solution.py:39
  6.2 7.8 %all-to-all-start = ((bf16[32,256,256]{2,1,0:T(8,128)(2,1)}), bf16[32,256,256]{2,1,0:T(8,128)(2,1)}, u32[]{:S(2)}, u32[]{:S(2)}) async-start(bf16[32,256,256]{2,1,0:T(8,128)(2,1)} %mask.1), calls=%async_computation | async-start | bytes 8388608 | tf_op jit(solution)/shard_map/all_to_all | solution.py:281
  14.1 0.5 places.1
  14.7 8.2 %collective-permute-start = (s16[8,8,1024]{2,1,0:T(8,128)(2,1)S(1)}, s16[8,8,1024]{2,1,0:T(8,128)(2,1)S(1)}, u32[]{:S(2)}, u32[]{:S(2)}) collective-permute-start(s16[8,8,1024]{2,1,0:T(8,128)(2,1)S(1)} %convert_element_type.65), channel_id=1, source_target_pairs={{0,0},{1,40},{2,8},{3,32},{4,16},{5,56},{6,24},{7,48},{8,33},{9,9}... | collective-permute-start | bytes 393224 | tf_op jit(solution)/shard_map/ppermute | solution.py:273
  22.9 2.7 %collective-permute-done = s16[8,8,1024]{2,1,0:T(8,128)(2,1)S(1)} collective-permute-done((s16[8,8,1024]{2,1,0:T(8,128)(2,1)S(1)}, s16[8,8,1024]{2,1,0:T(8,128)(2,1)S(1)}, u32[]{:S(2)}, u32[]{:S(2)}) %collective-permute-start) | collective-permute-done | bytes 131104 | tf_op jit(solution)/shard_map/ppermute | solution.py:273
  25.6 6.6 %collective-permute-start.1 = (s16[2,2,8,1024]{3,2,1,0:T(8,128)(2,1)S(1)}, s16[2,2,8,1024]{3,2,1,0:T(8,128)(2,1)S(1)}, u32[]{:S(2)}, u32[]{:S(2)}) collective-permute-start(s16[2,2,8,1024]{3,2,1,0:T(8,128)(2,1)S(1)} %bitcast.63), channel_id=1, source_target_pairs={{0,32},{8,40},{16,48},{24,56},{32,0},{40,8},{48,16},{56,24},{1,33}... | collective-permute-start | bytes 196616 | tf_op jit(solution)/shard_map/ppermute | solution.py:121
  32.2 1.7 %collective-permute-done.1 = s16[2,2,8,1024]{3,2,1,0:T(8,128)(2,1)S(1)} collective-permute-done((s16[2,2,8,1024]{3,2,1,0:T(8,128)(2,1)S(1)}, s16[2,2,8,1024]{3,2,1,0:T(8,128)(2,1)S(1)}, u32[]{:S(2)}, u32[]{:S(2)}) %collective-permute-start.1) | collective-permute-done | bytes 65568 | tf_op jit(solution)/shard_map/ppermute | solution.py:121
  34.0 5.7 %gather_fusion = f32[1024,256]{1,0:T(8,128)S(1)} fusion(f32[4096,256]{1,0:T(8,128)} %bitcast.56, s32[1024]{0:T(1024)S(1)} %broadcast_clamp_fusion), kind=kCustom, calls=%fused_computation | custom fusion | bytes 2101248 | tf_op jit(solution)/shard_map/jit(_take)/gather | solution.py:275
  39.7 3.0 %collective-permute-start.3 = (s16[2,2,8,1024]{3,2,1,0:T(8,128)(2,1)S(1)}, s16[2,2,8,1024]{3,2,1,0:T(8,128)(2,1)S(1)}, u32[]{:S(2)}, u32[]{:S(2)}) collective-permute-start(s16[2,2,8,1024]{3,2,1,0:T(8,128)(2,1)S(1)} %get-tuple-element.23), channel_id=1, source_target_pairs={{0,8},{8,0},{16,24},{24,16},{32,40},{40,32},{48,56},{56,48},{1,9},... | collective-permute-start | bytes 196616 | tf_op jit(solution)/shard_map/ppermute | solution.py:121
  43.1 1.7 %collective-permute-done.3 = s16[2,2,8,1024]{3,2,1,0:T(8,128)(2,1)S(1)} collective-permute-done((s16[2,2,8,1024]{3,2,1,0:T(8,128)(2,1)S(1)}, s16[2,2,8,1024]{3,2,1,0:T(8,128)(2,1)S(1)}, u32[]{:S(2)}, u32[]{:S(2)}) %collective-permute-start.3) | collective-permute-done | bytes 65568 | tf_op jit(solution)/shard_map/ppermute | solution.py:121
  44.8 0.7 convert_element_type.66.place_ref
  45.6 15.9 %counts.1.count_hbm = f8e4m3fn[8,1024,1024]{2,1,0:T(32,128)(4,1)} custom-call(s32[8,8,1024]{2,1,0:T(8,128)} %convert_element_type.66.place_ref), custom_call_target="tpu_custom_call" | custom-call | flops 201326592 | bytes 8388608 | tf_op jit(solution)/shard_map/counts/pallas_call | solution.py:178
  61.4 7.0 %all-to-all-done = bf16[32,256,256]{2,1,0:T(8,128)(2,1)} async-done(((bf16[32,256,256]{2,1,0:T(8,128)(2,1)}), bf16[32,256,256]{2,1,0:T(8,128)(2,1)}, u32[]{:S(2)}, u32[]{:S(2)}) %all-to-all-start) | async-done | bytes 4194336 | tf_op jit(solution)/shard_map/all_to_all | solution.py:281
  68.5 8.4 %plane_sum.1 = (bf16[3,128,256]{2,1,0:T(8,128)(2,1)}, bf16[2,128,256]{2,1,0:T(8,128)(2,1)}, bf16[2,128,256]{2,1,0:T(8,128)(2,1)}, bf16[128,256]{1,0:T(8,128)(2,1)}) custom-call(s32[1]{0:T(128)} %bitcast.22.z_ref, s32[1]{0:T(128)} %bitcast.23.rep_ref, f8e4m3fn[8,1024,1024]{2,1,0:T(32,128)(4,1)} %counts.1.count_hbm, bf16[8192,256]{1,0:T(8,128)(2,1)} %bitcast.24.bags_hbm), custom_call_target="tpu_custom_call" | custom-call | flops 4294967296 | bytes 12582912 | tf_op jit(solution)/shard_map/plane_sum/pallas_call | solution.py:238
  76.8 0.9 collective-permute-start.4
  77.7 0.7 collective-permute-start.6
  78.4 3.9 %collective-permute-start.5 = (bf16[128,256]{1,0:T(8,128)(2,1)}, bf16[128,256]{1,0:T(8,128)(2,1)S(1)}, u32[]{:S(2)}, u32[]{:S(2)}) collective-permute-start(bf16[128,256]{1,0:T(8,128)(2,1)} %get-tuple-element.13), channel_id=1, source_target_pairs={{0,32},{8,40},{16,48},{24,56},{32,0},{40,8},{48,16},{56,24},{1,33}... | collective-permute-start | bytes 196616 | tf_op jit(solution)/shard_map/ppermute | solution.py:128
  82.3 0.9 fusion.5
  83.2 2.1 %collective-permute-start.7 = (bf16[128,256]{1,0:T(8,128)(2,1)S(1)}, bf16[128,256]{1,0:T(8,128)(2,1)S(1)}, u32[]{:S(2)}, u32[]{:S(2)}) collective-permute-start(bf16[128,256]{1,0:T(8,128)(2,1)S(1)} %get-tuple-element.20), channel_id=1, source_target_pairs={{0,16},{8,24},{16,32},{24,40},{32,48},{40,56},{48,0},{56,8},{1,17}... | collective-permute-start | bytes 196616 | tf_op jit(solution)/shard_map/ppermute | solution.py:128
  85.7 0.5 collective-permute-done.5
  86.2 3.4 %collective-permute-done.7 = bf16[128,256]{1,0:T(8,128)(2,1)S(1)} collective-permute-done((bf16[128,256]{1,0:T(8,128)(2,1)S(1)}, bf16[128,256]{1,0:T(8,128)(2,1)S(1)}, u32[]{:S(2)}, u32[]{:S(2)}) %collective-permute-start.7) | collective-permute-done | bytes 65568 | tf_op jit(solution)/shard_map/ppermute | solution.py:128
  89.6 0.9 collective-permute-done.8
  90.5 0.9 fusion.4
  91.4 8.8 %collective-permute-start.9 = (bf16[128,256]{1,0:T(8,128)(2,1)S(1)}, bf16[128,256]{1,0:T(8,128)(2,1)S(1)}, u32[]{:S(2)}, u32[]{:S(2)}) collective-permute-start(bf16[128,256]{1,0:T(8,128)(2,1)S(1)} %fusion.4), channel_id=1, source_target_pairs={{0,0},{1,8},{2,16},{3,24},{4,32},{5,40},{6,48},{7,56},{8,1},{9,9},... | collective-permute-start | bytes 196616 | tf_op jit(solution)/shard_map/ppermute | solution.py:287
  100.3 1.9 %collective-permute-done.9 = bf16[128,256]{1,0:T(8,128)(2,1)S(1)} collective-permute-done((bf16[128,256]{1,0:T(8,128)(2,1)S(1)}, bf16[128,256]{1,0:T(8,128)(2,1)S(1)}, u32[]{:S(2)}, u32[]{:S(2)}) %collective-permute-start.9) | collective-permute-done | bytes 65568 | tf_op jit(solution)/shard_map/ppermute | solution.py:287
  102.2 3.8 %collective-permute-start.12 = (bf16[128,256]{1,0:T(8,128)(2,1)S(1)}, bf16[128,256]{1,0:T(8,128)(2,1)S(1)}, u32[]{:S(2)}, u32[]{:S(2)}) collective-permute-start(bf16[128,256]{1,0:T(8,128)(2,1)S(1)} %collective-permute-done.9), channel_id=1, source_target_pairs={{0,6},{2,0},{4,2},{6,4},{1,7},{3,1},{5,3},{7,5},{8,14},{10,8},{12,... | collective-permute-start | bytes 196616 | tf_op jit(solution)/shard_map/ppermute | solution.py:145
  106.0 0.6 collective-permute-start.10
  106.6 1.0 collective-permute-done.12
  107.6 3.1 %collective-permute-done.11 = bf16[128,256]{1,0:T(8,128)(2,1)S(1)} collective-permute-done((bf16[128,256]{1,0:T(8,128)(2,1)S(1)}, bf16[128,256]{1,0:T(8,128)(2,1)S(1)}, u32[]{:S(2)}, u32[]{:S(2)}) %collective-permute-start.11) | collective-permute-done | bytes 65568 | tf_op jit(solution)/shard_map/ppermute | solution.py:145
  111.1 9.8 %all_gather.4 = bf16[4,2,128,256]{3,2,1,0:T(8,128)(2,1)S(1)} all-gather(bf16[4,1,128,256]{3,2,1,0:T(8,128)(2,1)S(1)} %select_select_fusion), channel_id=1, replica_groups=mesh['y'=4,'z'=8,'x'=4,'core'=2] {'core'}, dimensions={1}, use_global_device_ids=true | all-gather | bytes 786432 | tf_op jit(solution)/shard_map/all_gather | solution.py:147
  121.2 0.6 sqrt_add_fusion
  121.8 1.2 fusion.1
  (30 shorter events, 1.6 us)
Async XLA Ops:
  6.2 7.9 %copy-start = (s32[8192,1,8]{0,2,1:T(8,128)S(1)}, s32[8192,1,8]{0,2,1:T(8,128)}, u32[]{:S(2)}) copy-start(s32[8192,1,8]{0,2,1:T(8,128)} %param.9) | copy-start | bytes 786436
  6.2 7.9 %copy-start.3 = (s32[1,1,512]{2,1,0:T(1,128)S(1)}, s32[1,1,512]{2,1,0:T(1,128)}, u32[]{:S(2)}) copy-start(s32[1,1,512]{2,1,0:T(1,128)} %param.10) | copy-start | bytes 6148
  6.2 16.6 %copy-start.1 = (s32[1,1024]{1,0:T(1,128)S(1)}, s32[1,1024]{1,0:T(1,128)}, u32[]{:S(2)}) copy-start(s32[1,1024]{1,0:T(1,128)} %param.11) | copy-start | bytes 12292
  6.2 62.2 %all-to-all-start = ((bf16[32,256,256]{2,1,0:T(8,128)(2,1)}), bf16[32,256,256]{2,1,0:T(8,128)(2,1)}, u32[]{:S(2)}, u32[]{:S(2)}) async-start(bf16[32,256,256]{2,1,0:T(8,128)(2,1)} %mask.1), calls=%async_computation | async-start | bytes 8388608 | tf_op jit(solution)/shard_map/all_to_all | solution.py:281
  14.7 10.9 %collective-permute-start = (s16[8,8,1024]{2,1,0:T(8,128)(2,1)S(1)}, s16[8,8,1024]{2,1,0:T(8,128)(2,1)S(1)}, u32[]{:S(2)}, u32[]{:S(2)}) collective-permute-start(s16[8,8,1024]{2,1,0:T(8,128)(2,1)S(1)} %convert_element_type.65), channel_id=1, source_target_pairs={{0,0},{1,40},{2,8},{3,32},{4,16},{5,56},{6,24},{7,48},{8,33},{9,9}... | collective-permute-start | bytes 393224 | tf_op jit(solution)/shard_map/ppermute | solution.py:273
  25.6 8.3 %collective-permute-start.1 = (s16[2,2,8,1024]{3,2,1,0:T(8,128)(2,1)S(1)}, s16[2,2,8,1024]{3,2,1,0:T(8,128)(2,1)S(1)}, u32[]{:S(2)}, u32[]{:S(2)}) collective-permute-start(s16[2,2,8,1024]{3,2,1,0:T(8,128)(2,1)S(1)} %bitcast.63), channel_id=1, source_target_pairs={{0,32},{8,40},{16,48},{24,56},{32,0},{40,8},{48,16},{56,24},{1,33}... | collective-permute-start | bytes 196616 | tf_op jit(solution)/shard_map/ppermute | solution.py:121
  33.9 5.8 %collective-permute-start.2 = (s16[2,2,8,1024]{3,2,0,1:T(8,128)(2,1)S(1)}, s16[2,2,8,1024]{3,2,0,1:T(8,128)(2,1)S(1)}, u32[]{:S(2)}, u32[]{:S(2)}) collective-permute-start(s16[2,2,8,1024]{3,2,0,1:T(8,128)(2,1)S(1)} %get-tuple-element.25), channel_id=1, source_target_pairs={{0,16},{8,24},{16,0},{24,8},{32,48},{40,56},{48,32},{56,40},{1,17}... | collective-permute-start | bytes 196616 | tf_op jit(solution)/shard_map/ppermute | solution.py:121
  34.0 9.0 %copy-start.2 = (f32[1,4096]{1,0:T(1,128)S(1)}, f32[1,4096]{1,0:T(1,128)}, u32[]{:S(2)}) copy-start(f32[1,4096]{1,0:T(1,128)} %param.13) | copy-start | bytes 49156
  39.7 5.1 %collective-permute-start.3 = (s16[2,2,8,1024]{3,2,1,0:T(8,128)(2,1)S(1)}, s16[2,2,8,1024]{3,2,1,0:T(8,128)(2,1)S(1)}, u32[]{:S(2)}, u32[]{:S(2)}) collective-permute-start(s16[2,2,8,1024]{3,2,1,0:T(8,128)(2,1)S(1)} %get-tuple-element.23), channel_id=1, source_target_pairs={{0,8},{8,0},{16,24},{24,16},{32,40},{40,32},{48,56},{56,48},{1,9},... | collective-permute-start | bytes 196616 | tf_op jit(solution)/shard_map/ppermute | solution.py:121
  76.8 5.5 %collective-permute-start.4 = (bf16[2,128,256]{2,1,0:T(8,128)(2,1)}, bf16[2,128,256]{2,1,0:T(8,128)(2,1)S(1)}, u32[]{:S(2)}, u32[]{:S(2)}) collective-permute-start(bf16[2,128,256]{2,1,0:T(8,128)(2,1)} %get-tuple-element.12), channel_id=1, source_target_pairs={{0,8},{8,16},{16,24},{24,32},{32,40},{40,48},{48,56},{56,0},{1,9},... | collective-permute-start | bytes 393224 | tf_op jit(solution)/shard_map/ppermute | solution.py:128
  77.7 4.6 %collective-permute-start.6 = (bf16[2,128,256]{2,1,0:T(8,128)(2,1)}, bf16[2,128,256]{2,1,0:T(8,128)(2,1)S(1)}, u32[]{:S(2)}, u32[]{:S(2)}) collective-permute-start(bf16[2,128,256]{2,1,0:T(8,128)(2,1)} %get-tuple-element.14), channel_id=1, source_target_pairs={{0,56},{8,0},{16,8},{24,16},{32,24},{40,32},{48,40},{56,48},{1,57}... | collective-permute-start | bytes 393224 | tf_op jit(solution)/shard_map/ppermute | solution.py:128
  78.4 7.8 %collective-permute-start.5 = (bf16[128,256]{1,0:T(8,128)(2,1)}, bf16[128,256]{1,0:T(8,128)(2,1)S(1)}, u32[]{:S(2)}, u32[]{:S(2)}) collective-permute-start(bf16[128,256]{1,0:T(8,128)(2,1)} %get-tuple-element.13), channel_id=1, source_target_pairs={{0,32},{8,40},{16,48},{24,56},{32,0},{40,8},{48,16},{56,24},{1,33}... | collective-permute-start | bytes 196616 | tf_op jit(solution)/shard_map/ppermute | solution.py:128
  83.2 6.4 %collective-permute-start.7 = (bf16[128,256]{1,0:T(8,128)(2,1)S(1)}, bf16[128,256]{1,0:T(8,128)(2,1)S(1)}, u32[]{:S(2)}, u32[]{:S(2)}) collective-permute-start(bf16[128,256]{1,0:T(8,128)(2,1)S(1)} %get-tuple-element.20), channel_id=1, source_target_pairs={{0,16},{8,24},{16,32},{24,40},{32,48},{40,56},{48,0},{56,8},{1,17}... | collective-permute-start | bytes 196616 | tf_op jit(solution)/shard_map/ppermute | solution.py:128
  85.3 5.2 %collective-permute-start.8 = (bf16[128,256]{1,0:T(8,128)(2,1)S(1)}, bf16[128,256]{1,0:T(8,128)(2,1)S(1)}, u32[]{:S(2)}, u32[]{:S(2)}) collective-permute-start(bf16[128,256]{1,0:T(8,128)(2,1)S(1)} %get-tuple-element.21), channel_id=1, source_target_pairs={{0,48},{8,56},{16,0},{24,8},{32,16},{40,24},{48,32},{56,40},{1,49}... | collective-permute-start | bytes 196616 | tf_op jit(solution)/shard_map/ppermute | solution.py:128
  91.4 10.8 %collective-permute-start.9 = (bf16[128,256]{1,0:T(8,128)(2,1)S(1)}, bf16[128,256]{1,0:T(8,128)(2,1)S(1)}, u32[]{:S(2)}, u32[]{:S(2)}) collective-permute-start(bf16[128,256]{1,0:T(8,128)(2,1)S(1)} %fusion.4), channel_id=1, source_target_pairs={{0,0},{1,8},{2,16},{3,24},{4,32},{5,40},{6,48},{7,56},{8,1},{9,9},... | collective-permute-start | bytes 196616 | tf_op jit(solution)/shard_map/ppermute | solution.py:287
  102.2 5.4 %collective-permute-start.12 = (bf16[128,256]{1,0:T(8,128)(2,1)S(1)}, bf16[128,256]{1,0:T(8,128)(2,1)S(1)}, u32[]{:S(2)}, u32[]{:S(2)}) collective-permute-start(bf16[128,256]{1,0:T(8,128)(2,1)S(1)} %collective-permute-done.9), channel_id=1, source_target_pairs={{0,6},{2,0},{4,2},{6,4},{1,7},{3,1},{5,3},{7,5},{8,14},{10,8},{12,... | collective-permute-start | bytes 196616 | tf_op jit(solution)/shard_map/ppermute | solution.py:145
  106.0 4.7 %collective-permute-start.11 = (bf16[128,256]{1,0:T(8,128)(2,1)S(1)}, bf16[128,256]{1,0:T(8,128)(2,1)S(1)}, u32[]{:S(2)}, u32[]{:S(2)}) collective-permute-start(bf16[128,256]{1,0:T(8,128)(2,1)S(1)} %collective-permute-done.9), channel_id=1, source_target_pairs={{0,4},{2,6},{4,0},{6,2},{1,5},{3,7},{5,1},{7,3},{8,12},{10,14},{12... | collective-permute-start | bytes 196616 | tf_op jit(solution)/shard_map/ppermute | solution.py:145
  106.0 5.0 %collective-permute-start.10 = (bf16[128,256]{1,0:T(8,128)(2,1)S(1)}, bf16[128,256]{1,0:T(8,128)(2,1)S(1)}, u32[]{:S(2)}, u32[]{:S(2)}) collective-permute-start(bf16[128,256]{1,0:T(8,128)(2,1)S(1)} %collective-permute-done.9), channel_id=1, source_target_pairs={{0,2},{2,4},{4,6},{6,0},{1,3},{3,5},{5,7},{7,1},{8,10},{10,12},{12... | collective-permute-start | bytes 196616 | tf_op jit(solution)/shard_map/ppermute | solution.py:145

commit v5 on v4

--- a/solution.py
+++ b/solution.py
@@ -173,55 +173,63 @@
     lax.fori_loop(0, samples // 128, lanes, 0)
 
 
-def counts_of(places, active):
+def counts_of(places, active, first, dtype):
     reps, slots, wide = places.shape
+    reps = reps // 2
     return pl.pallas_call(
         count_kernel,
         grid=(reps,),
-        in_specs=[pl.BlockSpec((1, slots, wide), lambda j: (j, 0, 0))],
+        in_specs=[pl.BlockSpec((1, slots, wide), lambda j: (first + j, 0, 0))],
         out_specs=pl.BlockSpec((1, active, wide), lambda j: (j, 0, 0)),
-        out_shape=jax.ShapeDtypeStruct((reps, active, wide), jnp.float8_e4m3fn),
+        out_shape=jax.ShapeDtypeStruct((reps, active, wide), dtype),
         compiler_params=pltpu.CompilerParams(vmem_limit_bytes=56 * MIB),
         cost_estimate=pl.CostEstimate(flops=active * wide * reps * slots * 3, bytes_accessed=active * wide * reps, transcendentals=0),
         name="counts",
     )(places)
 
 
-AHEAD = 4
-
-
-def plane_kernel(z_ref, rep_ref, count_hbm, bags_hbm, even_ref, up_ref, down_ref, across_ref, count_buf, bags_buf, total_ref, count_sem, bags_sem):
-    reps, _, samples = count_hbm.shape
+AHEAD = 3
+
+
+def plane_kernel(z_ref, rep_ref, small_hbm, large_hbm, bags_hbm, even_ref, up_ref, down_ref, across_ref, *scratch):
+    small_buf, large_buf, small_bags, large_bags, total_ref, sems = scratch
+    steps, _, samples = small_hbm.shape
     n_z, rows = 8, across_ref.shape[0]
 
-    def copies(j):
-        slot = lax.rem(j, AHEAD)
-        group = rep_ref[0] ^ from_turn(z_ref[0] ^ j ^ rep_ref[0])
-        start = pl.multiple_of(group * samples, samples)
-        return (
-            pltpu.make_async_copy(count_hbm.at[j], count_buf.at[slot], count_sem.at[slot]),
-            pltpu.make_async_copy(bags_hbm.at[pl.ds(start, samples), :], bags_buf.at[slot], bags_sem.at[slot]),
-        )
-
-    for j in range(AHEAD - 1):
-        for copy in copies(jnp.int32(j)):
+    def copies(i):
+        slot = lax.rem(i, AHEAD)
+        found = []
+        for part, (count_hbm, count_buf, bags_buf) in enumerate(
+            ((small_hbm, small_buf, small_bags), (large_hbm, large_buf, large_bags))
+        ):
+            group = rep_ref[0] ^ from_turn(z_ref[0] ^ (i + part * steps) ^ rep_ref[0])
+            bags = bags_hbm.at[pl.ds(pl.multiple_of(group * samples, samples), samples), :]
+            found.append(pltpu.make_async_copy(count_hbm.at[i], count_buf.at[slot], sems.at[2 * part, slot]))
+            found.append(pltpu.make_async_copy(bags, bags_buf.at[slot], sems.at[2 * part + 1, slot]))
+        return found
+
+    for i in range(AHEAD - 1):
+        for copy in copies(jnp.int32(i)):
             copy.start()
     total_ref[...] = jnp.zeros_like(total_ref)
 
-    def step(j, carry):
-        @pl.when(j + AHEAD - 1 < reps)
+    def step(i, carry):
+        @pl.when(i + AHEAD - 1 < steps)
         def _():
-            for copy in copies(j + AHEAD - 1):
+            for copy in copies(i + AHEAD - 1):
                 copy.start()
 
-        for copy in copies(j):
+        for copy in copies(i):
             copy.wait()
-        slot = lax.rem(j, AHEAD)
-        counts = count_buf[slot].astype(jnp.bfloat16)
-        total_ref[...] += jnp.dot(counts, bags_buf[slot], preferred_element_type=jnp.float32)
+        slot = lax.rem(i, AHEAD)
+        small = small_buf[slot].astype(jnp.bfloat16)
+        sums = jnp.dot(small, small_bags[slot], preferred_element_type=jnp.float32)
+        sums += jnp.dot(large_buf[slot], large_bags[slot], preferred_element_type=jnp.float32)
+        total_ref[...] += sums
         return carry
 
-    lax.fori_loop(0, reps, step, 0)
+    lax.fori_loop(0, steps, step, 0)
+
     def rows_for(k):
         first = pl.multiple_of(lax.rem(z_ref[0] + k, n_z) * rows, rows)
         return total_ref[pl.ds(first, rows), :].astype(jnp.bfloat16)
@@ -232,34 +240,30 @@
     across_ref[...] = rows_for(4)
 
 
-def plane_sum(z, rep, counts, bags, n_z):
-    reps, active, samples = counts.shape
+def plane_sum(z, rep, small, large, bags, n_z):
+    steps, active, samples = small.shape
     width = bags.shape[1]
     return pl.pallas_call(
         plane_kernel,
         out_shape=[jax.ShapeDtypeStruct(lead + (active // n_z, width), jnp.bfloat16) for lead in ((3,), (2,), (2,), ())],
-        in_specs=[
-            pl.BlockSpec(memory_space=pltpu.SMEM),
-            pl.BlockSpec(memory_space=pltpu.SMEM),
-            pl.BlockSpec(memory_space=pl.ANY),
-            pl.BlockSpec(memory_space=pl.ANY),
-        ],
+        in_specs=[pl.BlockSpec(memory_space=pltpu.SMEM)] * 2 + [pl.BlockSpec(memory_space=pl.ANY)] * 3,
         out_specs=[pl.BlockSpec(memory_space=pltpu.VMEM)] * 4,
         scratch_shapes=[
-            pltpu.VMEM((AHEAD, active, samples), counts.dtype),
+            pltpu.VMEM((AHEAD, active, samples), small.dtype),
+            pltpu.VMEM((AHEAD, active, samples), large.dtype),
+            pltpu.VMEM((AHEAD, samples, width), jnp.bfloat16),
             pltpu.VMEM((AHEAD, samples, width), jnp.bfloat16),
             pltpu.VMEM((active, width), jnp.float32),
-            pltpu.SemaphoreType.DMA((AHEAD,)),
-            pltpu.SemaphoreType.DMA((AHEAD,)),
+            pltpu.SemaphoreType.DMA((4, AHEAD)),
         ],
         compiler_params=pltpu.CompilerParams(vmem_limit_bytes=56 * MIB),
         cost_estimate=pl.CostEstimate(
-            flops=2 * reps * active * samples * width,
-            bytes_accessed=reps * samples * (active + 2 * width),
+            flops=4 * steps * active * samples * width,
+            bytes_accessed=steps * samples * (3 * active + 4 * width),
             transcendentals=0,
         ),
         name="plane_sum",
-    )(z, rep, counts, bags)
+    )(z, rep, small, large, bags)
 
 
 def local(n_z, n_rep, pooled_grad, present_count, members, rep_pos, row_ids, table, accum):
@@ -280,8 +284,9 @@
     masked = masked_by_table(n_z, pooled_grad, present_count)
     arrived = lax.all_to_all(masked, REP + ("y",), split_axis=0, concat_axis=0, tiled=True)
 
-    counts = counts_of(places, active)
-    partial = plane_sum(z.reshape(1), rep.reshape(1), counts, arrived.reshape(-1, width), n_z)
+    small = counts_of(places, active, 0, jnp.float8_e4m3fn)
+    large = counts_of(places, active, n_z // 2, jnp.bfloat16)
+    partial = plane_sum(z.reshape(1), rep.reshape(1), small, large, arrived.reshape(-1, width), n_z)
 
     part = sum_over_z(*partial, n_z)
     part = lax.ppermute(part, ("z",) + REP, swap)

time: 123 us -> 123 us (level)
  waiting for transfers between devices: 24.3 us -> 21.8 us
  Pallas kernels: 30.5 us -> 32.8 us
    all_to_all x1, waiting for transfers between devices: 7.03 us -> 4.52 us  [local(): lax.all_to_all(masked, REP + ('y',), split_axis=0, concat_axis=0, tiled=T...]
    pallas_call x1 -> x2, Pallas kernels: 15.9 us -> 18.4 us  [counts_of(): pl.pallas_call(count_kernel, grid=(reps,), in_specs=[pl.BlockSpec((1, slo...]
  transfers between devices with their start and end apart: 14 -> 14, of which waited for: 11 -> 11; matrix products, arithmetic and copies ran while one was open for 6% -> 6% of each run, Pallas kernels for 13% -> 16%
where the time goes in v5:
time: 123 us
  starting transfers between devices  46.8 us (38%)
  Pallas kernels  32.8 us (27%)
  waiting for transfers between devices  21.8 us (18%)
  blocking collectives  9.81 us (8%)
  local copies, waits for them, and re-layouts  5.68 us (5%)
  other arithmetic  4.96 us (4%)
    pallas_call x2, Pallas kernels, counts_of(): pl.pallas_call(count_kernel, grid=(reps,), in_specs=[pl.BlockSpec((1, slo...  18.4 us
    all_gather x1, blocking collectives, gather_over_rep(): lax.all_gather(rows, 'core', axis=1, tiled=False).reshape(-1, part.shape[1])  9.81 us
    ppermute x3, starting transfers between devices, exchange_over_z(): come = lax.ppermute(go, 'z', [(z, z ^ bit) for z in range(n_z)])  9.77 us
    ppermute x1, starting transfers between devices, local(): part = lax.ppermute(part, ('z',) + REP, swap)  8.84 us
    pallas_call x1, Pallas kernels, plane_sum(): pl.pallas_call(plane_kernel, out_shape=[jax.ShapeDtypeStruct(lead + (acti...  8.23 us
    ppermute x1, starting transfers between devices, local(): places = lax.ppermute(places, ('z',) + REP, spread)  8.17 us
    ppermute x5, starting transfers between devices, shift(): return lax.ppermute(array, 'z', [(a, (a + by) % n_z) for a in range(n_z)])  7.93 us
    all_to_all x1, starting transfers between devices, local(): lax.all_to_all(masked, REP + ('y',), split_axis=0, concat_axis=0, tiled=T...  7.82 us
  transfers between devices with their start and end apart: 14, of which 11 were waited for; matrix products, arithmetic and copies ran while one was open for 6% of the time, Pallas kernels for 16%

profile of v5, /device:TPU:89, one launch (start us, length us, event | category | flops | bytes accessed | tf_op | source)
XLA Modules:
  0.0 122.7 jit_solution(17545360922047530435)
XLA Ops:
  0.6 5.5 %mask.1 = bf16[32,256,256]{2,1,0:T(8,128)(2,1)} custom-call(s32[1,32]{1,0:T(1,128)} %count_ref.1, f32[256,32,256]{2,1,0:T(8,128)} %grad_ref.1), custom_call_target="tpu_custom_call" | custom-call | flops 2097152 | bytes 12582912 | tf_op jit(solution)/shard_map/mask/pallas_call | solution.py:39
  6.2 7.8 %all-to-all-start = ((bf16[32,256,256]{2,1,0:T(8,128)(2,1)}), bf16[32,256,256]{2,1,0:T(8,128)(2,1)}, u32[]{:S(2)}, u32[]{:S(2)}) async-start(bf16[32,256,256]{2,1,0:T(8,128)(2,1)} %mask.1), calls=%async_computation | async-start | bytes 8388608 | tf_op jit(solution)/shard_map/all_to_all | solution.py:285
  14.0 0.5 places.1
  14.6 8.2 %collective-permute-start = (s16[8,8,1024]{2,1,0:T(8,128)(2,1)S(1)}, s16[8,8,1024]{2,1,0:T(8,128)(2,1)S(1)}, u32[]{:S(2)}, u32[]{:S(2)}) collective-permute-start(s16[8,8,1024]{2,1,0:T(8,128)(2,1)S(1)} %convert_element_type.65), channel_id=1, source_target_pairs={{0,0},{1,40},{2,8},{3,32},{4,16},{5,56},{6,24},{7,48},{8,33},{9,9}... | collective-permute-start | bytes 393224 | tf_op jit(solution)/shard_map/ppermute | solution.py:277
  22.8 2.7 %collective-permute-done = s16[8,8,1024]{2,1,0:T(8,128)(2,1)S(1)} collective-permute-done((s16[8,8,1024]{2,1,0:T(8,128)(2,1)S(1)}, s16[8,8,1024]{2,1,0:T(8,128)(2,1)S(1)}, u32[]{:S(2)}, u32[]{:S(2)}) %collective-permute-start) | collective-permute-done | bytes 131104 | tf_op jit(solution)/shard_map/ppermute | solution.py:277
  25.5 6.6 %collective-permute-start.1 = (s16[2,2,8,1024]{3,2,1,0:T(8,128)(2,1)S(1)}, s16[2,2,8,1024]{3,2,1,0:T(8,128)(2,1)S(1)}, u32[]{:S(2)}, u32[]{:S(2)}) collective-permute-start(s16[2,2,8,1024]{3,2,1,0:T(8,128)(2,1)S(1)} %bitcast.63), channel_id=1, source_target_pairs={{0,32},{8,40},{16,48},{24,56},{32,0},{40,8},{48,16},{56,24},{1,33}... | collective-permute-start | bytes 196616 | tf_op jit(solution)/shard_map/ppermute | solution.py:121
  32.2 1.7 %collective-permute-done.1 = s16[2,2,8,1024]{3,2,1,0:T(8,128)(2,1)S(1)} collective-permute-done((s16[2,2,8,1024]{3,2,1,0:T(8,128)(2,1)S(1)}, s16[2,2,8,1024]{3,2,1,0:T(8,128)(2,1)S(1)}, u32[]{:S(2)}, u32[]{:S(2)}) %collective-permute-start.1) | collective-permute-done | bytes 65568 | tf_op jit(solution)/shard_map/ppermute | solution.py:121
  33.9 5.7 %gather_fusion = f32[1024,256]{1,0:T(8,128)S(1)} fusion(f32[4096,256]{1,0:T(8,128)} %bitcast.56, s32[1024]{0:T(1024)S(1)} %broadcast_clamp_fusion), kind=kCustom, calls=%fused_computation | custom fusion | bytes 2101248 | tf_op jit(solution)/shard_map/jit(_take)/gather | solution.py:279
  39.6 3.0 %collective-permute-start.3 = (s16[2,2,8,1024]{3,2,1,0:T(8,128)(2,1)S(1)}, s16[2,2,8,1024]{3,2,1,0:T(8,128)(2,1)S(1)}, u32[]{:S(2)}, u32[]{:S(2)}) collective-permute-start(s16[2,2,8,1024]{3,2,1,0:T(8,128)(2,1)S(1)} %get-tuple-element.23), channel_id=1, source_target_pairs={{0,8},{8,0},{16,24},{24,16},{32,40},{40,32},{48,56},{56,48},{1,9},... | collective-permute-start | bytes 196616 | tf_op jit(solution)/shard_map/ppermute | solution.py:121
  43.0 1.7 %collective-permute-done.3 = s16[2,2,8,1024]{3,2,1,0:T(8,128)(2,1)S(1)} collective-permute-done((s16[2,2,8,1024]{3,2,1,0:T(8,128)(2,1)S(1)}, s16[2,2,8,1024]{3,2,1,0:T(8,128)(2,1)S(1)}, u32[]{:S(2)}, u32[]{:S(2)}) %collective-permute-start.3) | collective-permute-done | bytes 65568 | tf_op jit(solution)/shard_map/ppermute | solution.py:121
  44.7 0.7 convert_element_type.66.place_ref
  45.5 8.8 %counts.2.small_hbm = f8e4m3fn[4,1024,1024]{2,1,0:T(32,128)(4,1)} custom-call(s32[8,8,1024]{2,1,0:T(8,128)} %convert_element_type.66.place_ref), custom_call_target="tpu_custom_call" | custom-call | flops 100663296 | bytes 4194304 | tf_op jit(solution)/shard_map/counts/pallas_call | solution.py:179
  54.2 9.6 %counts.3.large_hbm = bf16[4,1024,1024]{2,1,0:T(8,128)(2,1)} custom-call(s32[8,8,1024]{2,1,0:T(8,128)} %convert_element_type.66.place_ref), custom_call_target="tpu_custom_call" | custom-call | flops 100663296 | bytes 4194304 | tf_op jit(solution)/shard_map/counts/pallas_call | solution.py:179
  63.9 4.5 %all-to-all-done = bf16[32,256,256]{2,1,0:T(8,128)(2,1)} async-done(((bf16[32,256,256]{2,1,0:T(8,128)(2,1)}), bf16[32,256,256]{2,1,0:T(8,128)(2,1)}, u32[]{:S(2)}, u32[]{:S(2)}) %all-to-all-start) | async-done | bytes 4194336 | tf_op jit(solution)/shard_map/all_to_all | solution.py:285
  68.4 8.2 %plane_sum.1 = (bf16[3,128,256]{2,1,0:T(8,128)(2,1)}, bf16[2,128,256]{2,1,0:T(8,128)(2,1)}, bf16[2,128,256]{2,1,0:T(8,128)(2,1)}, bf16[128,256]{1,0:T(8,128)(2,1)}) custom-call(s32[1]{0:T(128)} %bitcast.22.z_ref, s32[1]{0:T(128)} %bitcast.23.rep_ref, f8e4m3fn[4,1024,1024]{2,1,0:T(32,128)(4,1)} %counts.2.small_hbm, bf16[4,1024,1024]{2,1,0:T(8,128)(2,1)} %counts.3.large_hbm, ...), custom_call_target="tpu_custom_call" | custom-call | flops 4294967296 | bytes 16777216 | tf_op jit(solution)/shard_map/plane_sum/pallas_call | solution.py:246
  76.6 0.9 collective-permute-start.4
  77.5 0.7 collective-permute-start.6
  78.2 3.9 %collective-permute-start.5 = (bf16[128,256]{1,0:T(8,128)(2,1)}, bf16[128,256]{1,0:T(8,128)(2,1)S(1)}, u32[]{:S(2)}, u32[]{:S(2)}) collective-permute-start(bf16[128,256]{1,0:T(8,128)(2,1)} %get-tuple-element.13), channel_id=1, source_target_pairs={{0,32},{8,40},{16,48},{24,56},{32,0},{40,8},{48,16},{56,24},{1,33}... | collective-permute-start | bytes 196616 | tf_op jit(solution)/shard_map/ppermute | solution.py:128
  82.1 0.9 fusion.5
  83.0 2.1 %collective-permute-start.7 = (bf16[128,256]{1,0:T(8,128)(2,1)S(1)}, bf16[128,256]{1,0:T(8,128)(2,1)S(1)}, u32[]{:S(2)}, u32[]{:S(2)}) collective-permute-start(bf16[128,256]{1,0:T(8,128)(2,1)S(1)} %get-tuple-element.20), channel_id=1, source_target_pairs={{0,16},{8,24},{16,32},{24,40},{32,48},{40,56},{48,0},{56,8},{1,17}... | collective-permute-start | bytes 196616 | tf_op jit(solution)/shard_map/ppermute | solution.py:128
  86.0 3.3 %collective-permute-done.7 = bf16[128,256]{1,0:T(8,128)(2,1)S(1)} collective-permute-done((bf16[128,256]{1,0:T(8,128)(2,1)S(1)}, bf16[128,256]{1,0:T(8,128)(2,1)S(1)}, u32[]{:S(2)}, u32[]{:S(2)}) %collective-permute-start.7) | collective-permute-done | bytes 65568 | tf_op jit(solution)/shard_map/ppermute | solution.py:128
  89.3 1.0 collective-permute-done.8
  90.3 0.9 fusion.4
  91.2 8.8 %collective-permute-start.9 = (bf16[128,256]{1,0:T(8,128)(2,1)S(1)}, bf16[128,256]{1,0:T(8,128)(2,1)S(1)}, u32[]{:S(2)}, u32[]{:S(2)}) collective-permute-start(bf16[128,256]{1,0:T(8,128)(2,1)S(1)} %fusion.4), channel_id=1, source_target_pairs={{0,0},{1,8},{2,16},{3,24},{4,32},{5,40},{6,48},{7,56},{8,1},{9,9},... | collective-permute-start | bytes 196616 | tf_op jit(solution)/shard_map/ppermute | solution.py:292
  100.1 1.9 %collective-permute-done.9 = bf16[128,256]{1,0:T(8,128)(2,1)S(1)} collective-permute-done((bf16[128,256]{1,0:T(8,128)(2,1)S(1)}, bf16[128,256]{1,0:T(8,128)(2,1)S(1)}, u32[]{:S(2)}, u32[]{:S(2)}) %collective-permute-start.9) | collective-permute-done | bytes 65568 | tf_op jit(solution)/shard_map/ppermute | solution.py:292
  102.0 3.7 %collective-permute-start.12 = (bf16[128,256]{1,0:T(8,128)(2,1)S(1)}, bf16[128,256]{1,0:T(8,128)(2,1)S(1)}, u32[]{:S(2)}, u32[]{:S(2)}) collective-permute-start(bf16[128,256]{1,0:T(8,128)(2,1)S(1)} %collective-permute-done.9), channel_id=1, source_target_pairs={{0,6},{2,0},{4,2},{6,4},{1,7},{3,1},{5,3},{7,5},{8,14},{10,8},{12,... | collective-permute-start | bytes 196616 | tf_op jit(solution)/shard_map/ppermute | solution.py:145
  105.7 0.6 collective-permute-start.10
  106.3 1.1 collective-permute-done.12
  107.4 3.0 %collective-permute-done.11 = bf16[128,256]{1,0:T(8,128)(2,1)S(1)} collective-permute-done((bf16[128,256]{1,0:T(8,128)(2,1)S(1)}, bf16[128,256]{1,0:T(8,128)(2,1)S(1)}, u32[]{:S(2)}, u32[]{:S(2)}) %collective-permute-start.11) | collective-permute-done | bytes 65568 | tf_op jit(solution)/shard_map/ppermute | solution.py:145
  110.9 9.8 %all_gather.4 = bf16[4,2,128,256]{3,2,1,0:T(8,128)(2,1)S(1)} all-gather(bf16[4,1,128,256]{3,2,1,0:T(8,128)(2,1)S(1)} %select_select_fusion), channel_id=1, replica_groups=mesh['y'=4,'z'=8,'x'=4,'core'=2] {'core'}, dimensions={1}, use_global_device_ids=true | all-gather | bytes 786432 | tf_op jit(solution)/shard_map/all_gather | solution.py:147
  120.9 0.6 sqrt_add_fusion
  121.5 1.2 fusion.1
  (31 shorter events, 2.1 us)
Async XLA Ops:
  6.2 7.9 %copy-start = (s32[8192,1,8]{0,2,1:T(8,128)S(1)}, s32[8192,1,8]{0,2,1:T(8,128)}, u32[]{:S(2)}) copy-start(s32[8192,1,8]{0,2,1:T(8,128)} %param.9) | copy-start | bytes 786436
  6.2 7.9 %copy-start.3 = (s32[1,1,512]{2,1,0:T(1,128)S(1)}, s32[1,1,512]{2,1,0:T(1,128)}, u32[]{:S(2)}) copy-start(s32[1,1,512]{2,1,0:T(1,128)} %param.10) | copy-start | bytes 6148
  6.2 16.6 %copy-start.1 = (s32[1,1024]{1,0:T(1,128)S(1)}, s32[1,1024]{1,0:T(1,128)}, u32[]{:S(2)}) copy-start(s32[1,1024]{1,0:T(1,128)} %param.11) | copy-start | bytes 12292
  6.2 62.2 %all-to-all-start = ((bf16[32,256,256]{2,1,0:T(8,128)(2,1)}), bf16[32,256,256]{2,1,0:T(8,128)(2,1)}, u32[]{:S(2)}, u32[]{:S(2)}) async-start(bf16[32,256,256]{2,1,0:T(8,128)(2,1)} %mask.1), calls=%async_computation | async-start | bytes 8388608 | tf_op jit(solution)/shard_map/all_to_all | solution.py:285
  14.6 10.9 %collective-permute-start = (s16[8,8,1024]{2,1,0:T(8,128)(2,1)S(1)}, s16[8,8,1024]{2,1,0:T(8,128)(2,1)S(1)}, u32[]{:S(2)}, u32[]{:S(2)}) collective-permute-start(s16[8,8,1024]{2,1,0:T(8,128)(2,1)S(1)} %convert_element_type.65), channel_id=1, source_target_pairs={{0,0},{1,40},{2,8},{3,32},{4,16},{5,56},{6,24},{7,48},{8,33},{9,9}... | collective-permute-start | bytes 393224 | tf_op jit(solution)/shard_map/ppermute | solution.py:277
  25.5 8.3 %collective-permute-start.1 = (s16[2,2,8,1024]{3,2,1,0:T(8,128)(2,1)S(1)}, s16[2,2,8,1024]{3,2,1,0:T(8,128)(2,1)S(1)}, u32[]{:S(2)}, u32[]{:S(2)}) collective-permute-start(s16[2,2,8,1024]{3,2,1,0:T(8,128)(2,1)S(1)} %bitcast.63), channel_id=1, source_target_pairs={{0,32},{8,40},{16,48},{24,56},{32,0},{40,8},{48,16},{56,24},{1,33}... | collective-permute-start | bytes 196616 | tf_op jit(solution)/shard_map/ppermute | solution.py:121
  33.8 5.8 %collective-permute-start.2 = (s16[2,2,8,1024]{3,2,0,1:T(8,128)(2,1)S(1)}, s16[2,2,8,1024]{3,2,0,1:T(8,128)(2,1)S(1)}, u32[]{:S(2)}, u32[]{:S(2)}) collective-permute-start(s16[2,2,8,1024]{3,2,0,1:T(8,128)(2,1)S(1)} %get-tuple-element.25), channel_id=1, source_target_pairs={{0,16},{8,24},{16,0},{24,8},{32,48},{40,56},{48,32},{56,40},{1,17}... | collective-permute-start | bytes 196616 | tf_op jit(solution)/shard_map/ppermute | solution.py:121
  33.9 9.0 %copy-start.2 = (f32[1,4096]{1,0:T(1,128)S(1)}, f32[1,4096]{1,0:T(1,128)}, u32[]{:S(2)}) copy-start(f32[1,4096]{1,0:T(1,128)} %param.13) | copy-start | bytes 49156
  39.6 5.1 %collective-permute-start.3 = (s16[2,2,8,1024]{3,2,1,0:T(8,128)(2,1)S(1)}, s16[2,2,8,1024]{3,2,1,0:T(8,128)(2,1)S(1)}, u32[]{:S(2)}, u32[]{:S(2)}) collective-permute-start(s16[2,2,8,1024]{3,2,1,0:T(8,128)(2,1)S(1)} %get-tuple-element.23), channel_id=1, source_target_pairs={{0,8},{8,0},{16,24},{24,16},{32,40},{40,32},{48,56},{56,48},{1,9},... | collective-permute-start | bytes 196616 | tf_op jit(solution)/shard_map/ppermute | solution.py:121
  76.6 5.5 %collective-permute-start.4 = (bf16[2,128,256]{2,1,0:T(8,128)(2,1)}, bf16[2,128,256]{2,1,0:T(8,128)(2,1)S(1)}, u32[]{:S(2)}, u32[]{:S(2)}) collective-permute-start(bf16[2,128,256]{2,1,0:T(8,128)(2,1)} %get-tuple-element.12), channel_id=1, source_target_pairs={{0,8},{8,16},{16,24},{24,32},{32,40},{40,48},{48,56},{56,0},{1,9},... | collective-permute-start | bytes 393224 | tf_op jit(solution)/shard_map/ppermute | solution.py:128
  77.5 4.6 %collective-permute-start.6 = (bf16[2,128,256]{2,1,0:T(8,128)(2,1)}, bf16[2,128,256]{2,1,0:T(8,128)(2,1)S(1)}, u32[]{:S(2)}, u32[]{:S(2)}) collective-permute-start(bf16[2,128,256]{2,1,0:T(8,128)(2,1)} %get-tuple-element.14), channel_id=1, source_target_pairs={{0,56},{8,0},{16,8},{24,16},{32,24},{40,32},{48,40},{56,48},{1,57}... | collective-permute-start | bytes 393224 | tf_op jit(solution)/shard_map/ppermute | solution.py:128
  78.2 7.8 %collective-permute-start.5 = (bf16[128,256]{1,0:T(8,128)(2,1)}, bf16[128,256]{1,0:T(8,128)(2,1)S(1)}, u32[]{:S(2)}, u32[]{:S(2)}) collective-permute-start(bf16[128,256]{1,0:T(8,128)(2,1)} %get-tuple-element.13), channel_id=1, source_target_pairs={{0,32},{8,40},{16,48},{24,56},{32,0},{40,8},{48,16},{56,24},{1,33}... | collective-permute-start | bytes 196616 | tf_op jit(solution)/shard_map/ppermute | solution.py:128
  83.0 6.3 %collective-permute-start.7 = (bf16[128,256]{1,0:T(8,128)(2,1)S(1)}, bf16[128,256]{1,0:T(8,128)(2,1)S(1)}, u32[]{:S(2)}, u32[]{:S(2)}) collective-permute-start(bf16[128,256]{1,0:T(8,128)(2,1)S(1)} %get-tuple-element.20), channel_id=1, source_target_pairs={{0,16},{8,24},{16,32},{24,40},{32,48},{40,56},{48,0},{56,8},{1,17}... | collective-permute-start | bytes 196616 | tf_op jit(solution)/shard_map/ppermute | solution.py:128
  85.1 5.2 %collective-permute-start.8 = (bf16[128,256]{1,0:T(8,128)(2,1)S(1)}, bf16[128,256]{1,0:T(8,128)(2,1)S(1)}, u32[]{:S(2)}, u32[]{:S(2)}) collective-permute-start(bf16[128,256]{1,0:T(8,128)(2,1)S(1)} %get-tuple-element.21), channel_id=1, source_target_pairs={{0,48},{8,56},{16,0},{24,8},{32,16},{40,24},{48,32},{56,40},{1,49}... | collective-permute-start | bytes 196616 | tf_op jit(solution)/shard_map/ppermute | solution.py:128
  91.2 10.8 %collective-permute-start.9 = (bf16[128,256]{1,0:T(8,128)(2,1)S(1)}, bf16[128,256]{1,0:T(8,128)(2,1)S(1)}, u32[]{:S(2)}, u32[]{:S(2)}) collective-permute-start(bf16[128,256]{1,0:T(8,128)(2,1)S(1)} %fusion.4), channel_id=1, source_target_pairs={{0,0},{1,8},{2,16},{3,24},{4,32},{5,40},{6,48},{7,56},{8,1},{9,9},... | collective-permute-start | bytes 196616 | tf_op jit(solution)/shard_map/ppermute | solution.py:292
  102.0 5.4 %collective-permute-start.12 = (bf16[128,256]{1,0:T(8,128)(2,1)S(1)}, bf16[128,256]{1,0:T(8,128)(2,1)S(1)}, u32[]{:S(2)}, u32[]{:S(2)}) collective-permute-start(bf16[128,256]{1,0:T(8,128)(2,1)S(1)} %collective-permute-done.9), channel_id=1, source_target_pairs={{0,6},{2,0},{4,2},{6,4},{1,7},{3,1},{5,3},{7,5},{8,14},{10,8},{12,... | collective-permute-start | bytes 196616 | tf_op jit(solution)/shard_map/ppermute | solution.py:145
  105.7 4.7 %collective-permute-start.11 = (bf16[128,256]{1,0:T(8,128)(2,1)S(1)}, bf16[128,256]{1,0:T(8,128)(2,1)S(1)}, u32[]{:S(2)}, u32[]{:S(2)}) collective-permute-start(bf16[128,256]{1,0:T(8,128)(2,1)S(1)} %collective-permute-done.9), channel_id=1, source_target_pairs={{0,4},{2,6},{4,0},{6,2},{1,5},{3,7},{5,1},{7,3},{8,12},{10,14},{12... | collective-permute-start | bytes 196616 | tf_op jit(solution)/shard_map/ppermute | solution.py:145
  105.7 5.0 %collective-permute-start.10 = (bf16[128,256]{1,0:T(8,128)(2,1)S(1)}, bf16[128,256]{1,0:T(8,128)(2,1)S(1)}, u32[]{:S(2)}, u32[]{:S(2)}) collective-permute-start(bf16[128,256]{1,0:T(8,128)(2,1)S(1)} %collective-permute-done.9), channel_id=1, source_target_pairs={{0,2},{2,4},{4,6},{6,0},{1,3},{3,5},{5,7},{7,1},{8,10},{10,12},{12... | collective-permute-start | bytes 196616 | tf_op jit(solution)/shard_map/ppermute | solution.py:145

commit v6 on v5

--- a/solution.py
+++ b/solution.py
@@ -130,9 +130,10 @@
     def plus(a, b):
         return a.astype(jnp.float32) + b.astype(jnp.float32)
 
-    up, down, across = shift(up, 1), shift(down, -1), shift(across, 4)
-    two_up = shift(plus(even[1], up[1]).astype(jnp.bfloat16), 2)
-    two_down = shift(plus(even[2], down[0]).astype(jnp.bfloat16), -2)
+    up, down = shift(up, 1), shift(down, -1)
+    two_up, two_down = plus(even[1], up[1]).astype(jnp.bfloat16), plus(even[2], down[0]).astype(jnp.bfloat16)
+    two_up, two_down, across = lax.optimization_barrier((two_up, two_down, across))
+    two_up, two_down, across = shift(two_up, 2), shift(two_down, -2), shift(across, 4)
     total = plus(even[0], up[0]) + plus(across, down[1]) + plus(two_up, two_down)
     return total.astype(jnp.bfloat16)
 

time: 123 us -> 125 us (1.016)
  the two profiles are of different devices: /device:TPU:89 before, /device:TPU:1 now
where the time goes in v6:
time: 125 us; the launch traced here: 124 us
  starting transfers between devices  55.4 us (44%)
  Pallas kernels  32.7 us (26%)
  waiting for transfers between devices  18.2 us (15%)
  blocking collectives  6.13 us (5%)
  local copies, waits for them, and re-layouts  5.68 us (5%)
  other arithmetic  4.96 us (4%)
    pallas_call x2, Pallas kernels, counts_of(): pl.pallas_call(count_kernel, grid=(reps,), in_specs=[pl.BlockSpec((1, slo...  18.4 us
    ppermute x5, starting transfers between devices, shift(): return lax.ppermute(array, 'z', [(a, (a + by) % n_z) for a in range(n_z)])  13.6 us
    ppermute x3, starting transfers between devices, exchange_over_z(): come = lax.ppermute(go, 'z', [(z, z ^ bit) for z in range(n_z)])  11.3 us
    all_to_all x1, starting transfers between devices, local(): lax.all_to_all(masked, REP + ('y',), split_axis=0, concat_axis=0, tiled=T...  8.79 us
    ppermute x1, starting transfers between devices, local(): places = lax.ppermute(places, ('z',) + REP, spread)  8.57 us
    pallas_call x1, Pallas kernels, plane_sum(): pl.pallas_call(plane_kernel, out_shape=[jax.ShapeDtypeStruct(lead + (acti...  8.17 us
    ppermute x1, starting transfers between devices, local(): part = lax.ppermute(part, ('z',) + REP, swap)  6.58 us
    ppermute x3, starting transfers between devices, gather_over_rep(): come = lax.ppermute(part, 'x', [(a, (a - step) % n_x) for a in range(n_x)])  6.5 us
  transfers between devices with their start and end apart: 14, of which 11 were waited for; matrix products, arithmetic and copies ran while one was open for 5% of the time, Pallas kernels for 15%

profile of v6, /device:TPU:1, one launch (start us, length us, event | category | flops | bytes accessed | tf_op | source)
XLA Modules:
  0.0 124.0 jit_solution(5553485856649518966)
XLA Ops:
  0.6 5.5 %mask.1 = bf16[32,256,256]{2,1,0:T(8,128)(2,1)} custom-call(s32[1,32]{1,0:T(1,128)} %count_ref.1, f32[256,32,256]{2,1,0:T(8,128)} %grad_ref.1), custom_call_target="tpu_custom_call" | custom-call | flops 2097152 | bytes 12582912 | tf_op jit(solution)/shard_map/mask/pallas_call | solution.py:39
  6.2 8.8 %all-to-all-start = ((bf16[32,256,256]{2,1,0:T(8,128)(2,1)}), bf16[32,256,256]{2,1,0:T(8,128)(2,1)}, u32[]{:S(2)}, u32[]{:S(2)}) async-start(bf16[32,256,256]{2,1,0:T(8,128)(2,1)} %mask.1), calls=%async_computation | async-start | bytes 8388608 | tf_op jit(solution)/shard_map/all_to_all | solution.py:286
  15.6 8.6 %collective-permute-start = (s16[8,8,1024]{2,1,0:T(8,128)(2,1)S(1)}, s16[8,8,1024]{2,1,0:T(8,128)(2,1)S(1)}, u32[]{:S(2)}, u32[]{:S(2)}) collective-permute-start(s16[8,8,1024]{2,1,0:T(8,128)(2,1)S(1)} %convert_element_type.65), channel_id=1, source_target_pairs={{0,0},{1,40},{2,8},{3,32},{4,16},{5,56},{6,24},{7,48},{8,33},{9,9}... | collective-permute-start | bytes 393224 | tf_op jit(solution)/shard_map/ppermute | solution.py:278
  24.2 1.9 %collective-permute-done = s16[8,8,1024]{2,1,0:T(8,128)(2,1)S(1)} collective-permute-done((s16[8,8,1024]{2,1,0:T(8,128)(2,1)S(1)}, s16[8,8,1024]{2,1,0:T(8,128)(2,1)S(1)}, u32[]{:S(2)}, u32[]{:S(2)}) %collective-permute-start) | collective-permute-done | bytes 131104 | tf_op jit(solution)/shard_map/ppermute | solution.py:278
  26.1 6.2 %collective-permute-start.1 = (s16[2,2,8,1024]{3,2,1,0:T(8,128)(2,1)S(1)}, s16[2,2,8,1024]{3,2,1,0:T(8,128)(2,1)S(1)}, u32[]{:S(2)}, u32[]{:S(2)}) collective-permute-start(s16[2,2,8,1024]{3,2,1,0:T(8,128)(2,1)S(1)} %bitcast.63), channel_id=1, source_target_pairs={{0,32},{8,40},{16,48},{24,56},{32,0},{40,8},{48,16},{56,24},{1,33}... | collective-permute-start | bytes 196616 | tf_op jit(solution)/shard_map/ppermute | solution.py:121
  32.3 2.1 %collective-permute-done.1 = s16[2,2,8,1024]{3,2,1,0:T(8,128)(2,1)S(1)} collective-permute-done((s16[2,2,8,1024]{3,2,1,0:T(8,128)(2,1)S(1)}, s16[2,2,8,1024]{3,2,1,0:T(8,128)(2,1)S(1)}, u32[]{:S(2)}, u32[]{:S(2)}) %collective-permute-start.1) | collective-permute-done | bytes 65568 | tf_op jit(solution)/shard_map/ppermute | solution.py:121
  34.4 4.2 %collective-permute-start.2 = (s16[2,2,8,1024]{3,2,0,1:T(8,128)(2,1)S(1)}, s16[2,2,8,1024]{3,2,0,1:T(8,128)(2,1)S(1)}, u32[]{:S(2)}, u32[]{:S(2)}) collective-permute-start(s16[2,2,8,1024]{3,2,0,1:T(8,128)(2,1)S(1)} %get-tuple-element.31), channel_id=1, source_target_pairs={{0,16},{8,24},{16,0},{24,8},{32,48},{40,56},{48,32},{56,40},{1,17}... | collective-permute-start | bytes 196616 | tf_op jit(solution)/shard_map/ppermute | solution.py:121
  38.6 5.7 %gather_fusion = f32[1024,256]{1,0:T(8,128)S(1)} fusion(f32[4096,256]{1,0:T(8,128)} %bitcast.56, s32[1024]{0:T(1024)S(1)} %broadcast_clamp_fusion), kind=kCustom, calls=%fused_computation | custom fusion | bytes 2101248 | tf_op jit(solution)/shard_map/jit(_take)/gather | solution.py:280
  44.3 0.9 collective-permute-start.3
  45.5 2.4 %collective-permute-done.3 = s16[2,2,8,1024]{3,2,1,0:T(8,128)(2,1)S(1)} collective-permute-done((s16[2,2,8,1024]{3,2,1,0:T(8,128)(2,1)S(1)}, s16[2,2,8,1024]{3,2,1,0:T(8,128)(2,1)S(1)}, u32[]{:S(2)}, u32[]{:S(2)}) %collective-permute-start.3) | collective-permute-done | bytes 65568 | tf_op jit(solution)/shard_map/ppermute | solution.py:121
  47.9 0.7 convert_element_type.66.place_ref
  48.7 8.8 %counts.2.small_hbm = f8e4m3fn[4,1024,1024]{2,1,0:T(32,128)(4,1)} custom-call(s32[8,8,1024]{2,1,0:T(8,128)} %convert_element_type.66.place_ref), custom_call_target="tpu_custom_call" | custom-call | flops 100663296 | bytes 4194304 | tf_op jit(solution)/shard_map/counts/pallas_call | solution.py:180
  57.4 9.6 %counts.3.large_hbm = bf16[4,1024,1024]{2,1,0:T(8,128)(2,1)} custom-call(s32[8,8,1024]{2,1,0:T(8,128)} %convert_element_type.66.place_ref), custom_call_target="tpu_custom_call" | custom-call | flops 100663296 | bytes 4194304 | tf_op jit(solution)/shard_map/counts/pallas_call | solution.py:180
  67.1 8.2 %plane_sum.1 = (bf16[3,128,256]{2,1,0:T(8,128)(2,1)}, bf16[2,128,256]{2,1,0:T(8,128)(2,1)}, bf16[2,128,256]{2,1,0:T(8,128)(2,1)}, bf16[128,256]{1,0:T(8,128)(2,1)}) custom-call(s32[1]{0:T(128)} %bitcast.22.z_ref, s32[1]{0:T(128)} %bitcast.23.rep_ref, f8e4m3fn[4,1024,1024]{2,1,0:T(32,128)(4,1)} %counts.2.small_hbm, bf16[4,1024,1024]{2,1,0:T(8,128)(2,1)} %counts.3.large_hbm, ...), custom_call_target="tpu_custom_call" | custom-call | flops 4294967296 | bytes 16777216 | tf_op jit(solution)/shard_map/plane_sum/pallas_call | solution.py:247
  75.3 1.7 %collective-permute-start.4 = (bf16[2,128,256]{2,1,0:T(8,128)(2,1)}, bf16[2,128,256]{2,1,0:T(8,128)(2,1)S(1)}, u32[]{:S(2)}, u32[]{:S(2)}) collective-permute-start(bf16[2,128,256]{2,1,0:T(8,128)(2,1)} %get-tuple-element.15), channel_id=1, source_target_pairs={{0,8},{8,16},{16,24},{24,32},{32,40},{40,48},{48,56},{56,0},{1,9},... | collective-permute-start | bytes 393224 | tf_op jit(solution)/shard_map/ppermute | solution.py:128
  77.0 5.3 %collective-permute-start.5 = (bf16[2,128,256]{2,1,0:T(8,128)(2,1)}, bf16[2,128,256]{2,1,0:T(8,128)(2,1)S(1)}, u32[]{:S(2)}, u32[]{:S(2)}) collective-permute-start(bf16[2,128,256]{2,1,0:T(8,128)(2,1)} %get-tuple-element.16), channel_id=1, source_target_pairs={{0,56},{8,0},{16,8},{24,16},{32,24},{40,32},{48,40},{56,48},{1,57}... | collective-permute-start | bytes 393224 | tf_op jit(solution)/shard_map/ppermute | solution.py:128
  82.2 3.1 %collective-permute-done.4 = bf16[2,128,256]{2,1,0:T(8,128)(2,1)S(1)} collective-permute-done((bf16[2,128,256]{2,1,0:T(8,128)(2,1)}, bf16[2,128,256]{2,1,0:T(8,128)(2,1)S(1)}, u32[]{:S(2)}, u32[]{:S(2)}) %collective-permute-start.4) | collective-permute-done | bytes 131104 | tf_op jit(solution)/shard_map/ppermute | solution.py:128
  85.3 0.9 fusion.6
  86.3 3.1 %collective-permute-start.6 = (bf16[128,256]{1,0:T(8,128)(2,1)}, bf16[128,256]{1,0:T(8,128)(2,1)S(1)}, u32[]{:S(2)}, u32[]{:S(2)}) collective-permute-start(bf16[128,256]{1,0:T(8,128)(2,1)} %get-tuple-element.18), channel_id=1, source_target_pairs={{0,32},{8,40},{16,48},{24,56},{32,0},{40,8},{48,16},{56,24},{1,33}... | collective-permute-start | bytes 196616 | tf_op jit(solution)/shard_map/ppermute | solution.py:128
  89.3 1.4 %collective-permute-start.7 = (bf16[128,256]{1,0:T(8,128)(2,1)S(1)}, bf16[128,256]{1,0:T(8,128)(2,1)S(1)}, u32[]{:S(2)}, u32[]{:S(2)}) collective-permute-start(bf16[128,256]{1,0:T(8,128)(2,1)S(1)} %get-tuple-element.19), channel_id=1, source_target_pairs={{0,16},{8,24},{16,32},{24,40},{32,48},{40,56},{48,0},{56,8},{1,17}... | collective-permute-start | bytes 196616 | tf_op jit(solution)/shard_map/ppermute | solution.py:128
  90.7 2.2 %collective-permute-start.8 = (bf16[128,256]{1,0:T(8,128)(2,1)S(1)}, bf16[128,256]{1,0:T(8,128)(2,1)S(1)}, u32[]{:S(2)}, u32[]{:S(2)}) collective-permute-start(bf16[128,256]{1,0:T(8,128)(2,1)S(1)} %get-tuple-element.20), channel_id=1, source_target_pairs={{0,48},{8,56},{16,0},{24,8},{32,16},{40,24},{48,32},{56,40},{1,49}... | collective-permute-start | bytes 196616 | tf_op jit(solution)/shard_map/ppermute | solution.py:128
  92.9 0.8 collective-permute-done.6
  93.7 1.0 collective-permute-done.7
  94.7 0.6 collective-permute-done.8
  95.3 0.9 fusion.4
  96.2 6.6 %collective-permute-start.9 = (bf16[128,256]{1,0:T(8,128)(2,1)S(1)}, bf16[128,256]{1,0:T(8,128)(2,1)S(1)}, u32[]{:S(2)}, u32[]{:S(2)}) collective-permute-start(bf16[128,256]{1,0:T(8,128)(2,1)S(1)} %fusion.4), channel_id=1, source_target_pairs={{0,0},{1,8},{2,16},{3,24},{4,32},{5,40},{6,48},{7,56},{8,1},{9,9},... | collective-permute-start | bytes 196616 | tf_op jit(solution)/shard_map/ppermute | solution.py:293
  102.8 1.9 %collective-permute-done.9 = bf16[128,256]{1,0:T(8,128)(2,1)S(1)} collective-permute-done((bf16[128,256]{1,0:T(8,128)(2,1)S(1)}, bf16[128,256]{1,0:T(8,128)(2,1)S(1)}, u32[]{:S(2)}, u32[]{:S(2)}) %collective-permute-start.9) | collective-permute-done | bytes 65568 | tf_op jit(solution)/shard_map/ppermute | solution.py:293
  104.7 5.9 %collective-permute-start.12 = (bf16[128,256]{1,0:T(8,128)(2,1)S(1)}, bf16[128,256]{1,0:T(8,128)(2,1)S(1)}, u32[]{:S(2)}, u32[]{:S(2)}) collective-permute-start(bf16[128,256]{1,0:T(8,128)(2,1)S(1)} %collective-permute-done.9), channel_id=1, source_target_pairs={{0,6},{2,0},{4,2},{6,4},{1,7},{3,1},{5,3},{7,5},{8,14},{10,8},{12,... | collective-permute-start | bytes 196616 | tf_op jit(solution)/shard_map/ppermute | solution.py:146
  111.3 1.3 %collective-permute-done.12 = bf16[128,256]{1,0:T(8,128)(2,1)S(1)} collective-permute-done((bf16[128,256]{1,0:T(8,128)(2,1)S(1)}, bf16[128,256]{1,0:T(8,128)(2,1)S(1)}, u32[]{:S(2)}, u32[]{:S(2)}) %collective-permute-start.12) | collective-permute-done | bytes 65568 | tf_op jit(solution)/shard_map/ppermute | solution.py:146
  112.6 2.8 %collective-permute-done.11 = bf16[128,256]{1,0:T(8,128)(2,1)S(1)} collective-permute-done((bf16[128,256]{1,0:T(8,128)(2,1)S(1)}, bf16[128,256]{1,0:T(8,128)(2,1)S(1)}, u32[]{:S(2)}, u32[]{:S(2)}) %collective-permute-start.11) | collective-permute-done | bytes 65568 | tf_op jit(solution)/shard_map/ppermute | solution.py:146
  115.8 6.1 %all_gather.4 = bf16[4,2,128,256]{3,2,1,0:T(8,128)(2,1)S(1)} all-gather(bf16[4,1,128,256]{3,2,1,0:T(8,128)(2,1)S(1)} %select_select_fusion), channel_id=1, replica_groups=mesh['y'=4,'z'=8,'x'=4,'core'=2] {'core'}, dimensions={1}, use_global_device_ids=true | all-gather | bytes 786432 | tf_op jit(solution)/shard_map/all_gather | solution.py:148
  122.8 1.2 fusion.1
  (31 shorter events, 2.8 us)
Async XLA Ops:
  6.2 8.8 %copy-start = (s32[8192,1,8]{0,2,1:T(8,128)S(1)}, s32[8192,1,8]{0,2,1:T(8,128)}, u32[]{:S(2)}) copy-start(s32[8192,1,8]{0,2,1:T(8,128)} %param.9) | copy-start | bytes 786436
  6.2 8.8 %copy-start.3 = (s32[1,1,512]{2,1,0:T(1,128)S(1)}, s32[1,1,512]{2,1,0:T(1,128)}, u32[]{:S(2)}) copy-start(s32[1,1,512]{2,1,0:T(1,128)} %param.10) | copy-start | bytes 6148
  6.2 18.0 %copy-start.1 = (s32[1,1024]{1,0:T(1,128)S(1)}, s32[1,1024]{1,0:T(1,128)}, u32[]{:S(2)}) copy-start(s32[1,1024]{1,0:T(1,128)} %param.11) | copy-start | bytes 12292
  6.2 60.9 %all-to-all-start = ((bf16[32,256,256]{2,1,0:T(8,128)(2,1)}), bf16[32,256,256]{2,1,0:T(8,128)(2,1)}, u32[]{:S(2)}, u32[]{:S(2)}) async-start(bf16[32,256,256]{2,1,0:T(8,128)(2,1)} %mask.1), calls=%async_computation | async-start | bytes 8388608 | tf_op jit(solution)/shard_map/all_to_all | solution.py:286
  15.6 10.5 %collective-permute-start = (s16[8,8,1024]{2,1,0:T(8,128)(2,1)S(1)}, s16[8,8,1024]{2,1,0:T(8,128)(2,1)S(1)}, u32[]{:S(2)}, u32[]{:S(2)}) collective-permute-start(s16[8,8,1024]{2,1,0:T(8,128)(2,1)S(1)} %convert_element_type.65), channel_id=1, source_target_pairs={{0,0},{1,40},{2,8},{3,32},{4,16},{5,56},{6,24},{7,48},{8,33},{9,9}... | collective-permute-start | bytes 393224 | tf_op jit(solution)/shard_map/ppermute | solution.py:278
  26.1 8.2 %collective-permute-start.1 = (s16[2,2,8,1024]{3,2,1,0:T(8,128)(2,1)S(1)}, s16[2,2,8,1024]{3,2,1,0:T(8,128)(2,1)S(1)}, u32[]{:S(2)}, u32[]{:S(2)}) collective-permute-start(s16[2,2,8,1024]{3,2,1,0:T(8,128)(2,1)S(1)} %bitcast.63), channel_id=1, source_target_pairs={{0,32},{8,40},{16,48},{24,56},{32,0},{40,8},{48,16},{56,24},{1,33}... | collective-permute-start | bytes 196616 | tf_op jit(solution)/shard_map/ppermute | solution.py:121
  34.4 9.9 %collective-permute-start.2 = (s16[2,2,8,1024]{3,2,0,1:T(8,128)(2,1)S(1)}, s16[2,2,8,1024]{3,2,0,1:T(8,128)(2,1)S(1)}, u32[]{:S(2)}, u32[]{:S(2)}) collective-permute-start(s16[2,2,8,1024]{3,2,0,1:T(8,128)(2,1)S(1)} %get-tuple-element.31), channel_id=1, source_target_pairs={{0,16},{8,24},{16,0},{24,8},{32,48},{40,56},{48,32},{56,40},{1,17}... | collective-permute-start | bytes 196616 | tf_op jit(solution)/shard_map/ppermute | solution.py:121
  38.6 6.8 %copy-start.2 = (f32[1,4096]{1,0:T(1,128)S(1)}, f32[1,4096]{1,0:T(1,128)}, u32[]{:S(2)}) copy-start(f32[1,4096]{1,0:T(1,128)} %param.13) | copy-start | bytes 49156
  44.3 3.6 %collective-permute-start.3 = (s16[2,2,8,1024]{3,2,1,0:T(8,128)(2,1)S(1)}, s16[2,2,8,1024]{3,2,1,0:T(8,128)(2,1)S(1)}, u32[]{:S(2)}, u32[]{:S(2)}) collective-permute-start(s16[2,2,8,1024]{3,2,1,0:T(8,128)(2,1)S(1)} %get-tuple-element.29), channel_id=1, source_target_pairs={{0,8},{8,0},{16,24},{24,16},{32,40},{40,32},{48,56},{56,48},{1,9},... | collective-permute-start | bytes 196616 | tf_op jit(solution)/shard_map/ppermute | solution.py:121
  75.3 10.1 %collective-permute-start.4 = (bf16[2,128,256]{2,1,0:T(8,128)(2,1)}, bf16[2,128,256]{2,1,0:T(8,128)(2,1)S(1)}, u32[]{:S(2)}, u32[]{:S(2)}) collective-permute-start(bf16[2,128,256]{2,1,0:T(8,128)(2,1)} %get-tuple-element.15), channel_id=1, source_target_pairs={{0,8},{8,16},{16,24},{24,32},{32,40},{40,48},{48,56},{56,0},{1,9},... | collective-permute-start | bytes 393224 | tf_op jit(solution)/shard_map/ppermute | solution.py:128
  77.0 8.4 %collective-permute-start.5 = (bf16[2,128,256]{2,1,0:T(8,128)(2,1)}, bf16[2,128,256]{2,1,0:T(8,128)(2,1)S(1)}, u32[]{:S(2)}, u32[]{:S(2)}) collective-permute-start(bf16[2,128,256]{2,1,0:T(8,128)(2,1)} %get-tuple-element.16), channel_id=1, source_target_pairs={{0,56},{8,0},{16,8},{24,16},{32,24},{40,32},{48,40},{56,48},{1,57}... | collective-permute-start | bytes 393224 | tf_op jit(solution)/shard_map/ppermute | solution.py:128
  86.3 7.4 %collective-permute-start.6 = (bf16[128,256]{1,0:T(8,128)(2,1)}, bf16[128,256]{1,0:T(8,128)(2,1)S(1)}, u32[]{:S(2)}, u32[]{:S(2)}) collective-permute-start(bf16[128,256]{1,0:T(8,128)(2,1)} %get-tuple-element.18), channel_id=1, source_target_pairs={{0,32},{8,40},{16,48},{24,56},{32,0},{40,8},{48,16},{56,24},{1,33}... | collective-permute-start | bytes 196616 | tf_op jit(solution)/shard_map/ppermute | solution.py:128
  89.3 5.3 %collective-permute-start.7 = (bf16[128,256]{1,0:T(8,128)(2,1)S(1)}, bf16[128,256]{1,0:T(8,128)(2,1)S(1)}, u32[]{:S(2)}, u32[]{:S(2)}) collective-permute-start(bf16[128,256]{1,0:T(8,128)(2,1)S(1)} %get-tuple-element.19), channel_id=1, source_target_pairs={{0,16},{8,24},{16,32},{24,40},{32,48},{40,56},{48,0},{56,8},{1,17}... | collective-permute-start | bytes 196616 | tf_op jit(solution)/shard_map/ppermute | solution.py:128
  90.7 4.6 %collective-permute-start.8 = (bf16[128,256]{1,0:T(8,128)(2,1)S(1)}, bf16[128,256]{1,0:T(8,128)(2,1)S(1)}, u32[]{:S(2)}, u32[]{:S(2)}) collective-permute-start(bf16[128,256]{1,0:T(8,128)(2,1)S(1)} %get-tuple-element.20), channel_id=1, source_target_pairs={{0,48},{8,56},{16,0},{24,8},{32,16},{40,24},{48,32},{56,40},{1,49}... | collective-permute-start | bytes 196616 | tf_op jit(solution)/shard_map/ppermute | solution.py:128
  96.2 8.5 %collective-permute-start.9 = (bf16[128,256]{1,0:T(8,128)(2,1)S(1)}, bf16[128,256]{1,0:T(8,128)(2,1)S(1)}, u32[]{:S(2)}, u32[]{:S(2)}) collective-permute-start(bf16[128,256]{1,0:T(8,128)(2,1)S(1)} %fusion.4), channel_id=1, source_target_pairs={{0,0},{1,8},{2,16},{3,24},{4,32},{5,40},{6,48},{7,56},{8,1},{9,9},... | collective-permute-start | bytes 196616 | tf_op jit(solution)/shard_map/ppermute | solution.py:293
  104.7 7.8 %collective-permute-start.12 = (bf16[128,256]{1,0:T(8,128)(2,1)S(1)}, bf16[128,256]{1,0:T(8,128)(2,1)S(1)}, u32[]{:S(2)}, u32[]{:S(2)}) collective-permute-start(bf16[128,256]{1,0:T(8,128)(2,1)S(1)} %collective-permute-done.9), channel_id=1, source_target_pairs={{0,6},{2,0},{4,2},{6,4},{1,7},{3,1},{5,3},{7,5},{8,14},{10,8},{12,... | collective-permute-start | bytes 196616 | tf_op jit(solution)/shard_map/ppermute | solution.py:146
  110.7 4.7 %collective-permute-start.11 = (bf16[128,256]{1,0:T(8,128)(2,1)S(1)}, bf16[128,256]{1,0:T(8,128)(2,1)S(1)}, u32[]{:S(2)}, u32[]{:S(2)}) collective-permute-start(bf16[128,256]{1,0:T(8,128)(2,1)S(1)} %collective-permute-done.9), channel_id=1, source_target_pairs={{0,4},{2,6},{4,0},{6,2},{1,5},{3,7},{5,1},{7,3},{8,12},{10,14},{12... | collective-permute-start | bytes 196616 | tf_op jit(solution)/shard_map/ppermute | solution.py:146
  110.7 5.0 %collective-permute-start.10 = (bf16[128,256]{1,0:T(8,128)(2,1)S(1)}, bf16[128,256]{1,0:T(8,128)(2,1)S(1)}, u32[]{:S(2)}, u32[]{:S(2)}) collective-permute-start(bf16[128,256]{1,0:T(8,128)(2,1)S(1)} %collective-permute-done.9), channel_id=1, source_target_pairs={{0,2},{2,4},{4,6},{6,0},{1,3},{3,5},{5,7},{7,1},{8,10},{10,12},{12... | collective-permute-start | bytes 196616 | tf_op jit(solution)/shard_map/ppermute | solution.py:146
